TPU v7x, 32 devices: a whole 2x2x4 slice. The times are simulated.
32 devices in a mesh: gx: 2 (over x), gy: 4 (over y, core), gz: 4 (over z).
Axes of the slice: x: 2, y: 2, z: 4, core: 2. Of those that a mesh axis runs over, the one named last changes fastest.
Arguments:
- scalar_feat: bfloat16 [32000, 128], P(('gx', 'gy', 'gz')), may hold values from -6 to 6
- vector_feat: bfloat16 [32000, 384], P(('gx', 'gy', 'gz')), may hold values from -6 to 6
- positions: float32 [3, 32000], P(None, ('gx', 'gy', 'gz')), may hold values from 0 to 26, as said below
- message_inner: bfloat16 [128, 128], replicated, may hold values from -0.5 to 0.5
- message_inner_bias: float32 [128], replicated, may hold values from -3 to 3
- message_outer: bfloat16 [128, 384], replicated, may hold values from -0.5 to 0.5
- message_outer_bias: float32 [384], replicated, may hold values from -3 to 3
- radial_weight: bfloat16 [20, 384], replicated, may hold values from -2.5 to 2.5
- radial_bias: float32 [384], replicated, may hold values from -2 to 2
- update_left: bfloat16 [128, 128], replicated, may hold values from -0.5 to 0.5
- update_right: bfloat16 [128, 128], replicated, may hold values from -0.5 to 0.5
- update_inner: bfloat16 [256, 128], replicated, may hold values from -0.375 to 0.375
- update_inner_bias: float32 [128], replicated, may hold values from -3 to 3
- update_outer: bfloat16 [128, 384], replicated, may hold values from -0.5 to 0.5
- update_outer_bias: float32 [384], replicated, may hold values from -3 to 3
- scalar_cotangent: bfloat16 [32000, 128], P(('gx', 'gy', 'gz')), may hold values from -6 to 6
- vector_cotangent: bfloat16 [32000, 384], P(('gx', 'gy', 'gz')), may hold values from -6 to 6
- x_face_rows: int32 [32, 2, 100], P(('gx', 'gy', 'gz')), may hold values from 0 to 999, as said below
- y_face_rows: int32 [32, 2, 120], P(('gx', 'gy', 'gz')), may hold values from 0 to 1199, as said below
- z_face_rows: int32 [32, 2, 144], P(('gx', 'gy', 'gz')), may hold values from 0 to 1439, as said below
- neighbour_table: int32 [15, 32000], P(None, ('gx', 'gy', 'gz')), may hold values from 0 to 1727, as said below
- hub_atoms: int32 [4096], P(('gx', 'gy', 'gz')), may hold values from 0 to 999, as said below
- hub_table: int32 [11, 4096], P(None, ('gx', 'gy', 'gz')), may hold values from 0 to 1727, as said below
- hub_count: int32 [32], P(('gx', 'gy', 'gz')), may hold values from 32 to 128, as said below
Outputs:
- scalar_out: bfloat16 [32000, 128], P(('gx', 'gy', 'gz'))
- vector_out: bfloat16 [32000, 384], P(('gx', 'gy', 'gz'))
- scalar_grad: float32 [32000, 128], P(('gx', 'gy', 'gz'))
- vector_grad: float32 [32000, 384], P(('gx', 'gy', 'gz'))
- positions_grad: float32 [3, 32000], P(None, ('gx', 'gy', 'gz'))
- message_inner_grad: float32 [128, 128], replicated
- message_inner_bias_grad: float32 [128], replicated
- message_outer_grad: float32 [128, 384], replicated
- message_outer_bias_grad: float32 [384], replicated
- radial_weight_grad: float32 [20, 384], replicated
- radial_bias_grad: float32 [384], replicated
- update_left_grad: float32 [128, 128], replicated
- update_right_grad: float32 [128, 128], replicated
- update_inner_grad: float32 [256, 128], replicated
- update_inner_bias_grad: float32 [128], replicated
- update_outer_grad: float32 [128, 384], replicated
- update_outer_bias_grad: float32 [384], replicated
Inputs may be any that keep to these rules, and one draw needn't show every extreme that they name: `x_face_rows`: within a cell each own row appears at most once in each list. `y_face_rows`: entries index a cell's own rows and its x halo rows. `z_face_rows`: entries index a cell's own rows, x halo and y halo rows. `neighbour_table`: an atom's 15 entries are distinct and never its own row. `hub_atoms`: the atoms of one cell's hub slots are distinct. `hub_table`: A hub's entries are distinct, never its own row, and never among its neighbour_table entries. `hub_count`: some cell has all 128 slots live. `positions`: coordinates within the owning cell; an atom and each row that lists it as a neighbour lie 2 or more apart.
All inputs are finite; a program needn't handle non-finite values.
Results may differ from a plain program's by a relative error of at most 0.0089.
Values sent between devices are 32-bit elements; how exact they have to be, the bound alone decides.
No kernel may reach another device: no remote copies, remote signals or barrier semaphores. Data moves between devices by JAX's collectives and lax.ppermute only.
A program may use at most 128 MiB of HBM per device.

v0:
```python
import math

import jax
import jax.numpy as jnp
from jax import lax
from jax.sharding import PartitionSpec as P

G = 10


SPACING = 2.6
CUTOFF = 5.0
HIGH = lax.Precision.HIGHEST


def with_halo(x, sides, width):
    for axis, dim in sides:
        count, length = (lax.axis_size(axis), x.shape[dim])
        up = [(i, (i + 1) % count) for i in range(count)]
        down = [(j, i) for i, j in up]
        last = lax.slice_in_dim(x, length - width, length, axis=dim)
        first = lax.slice_in_dim(x, 0, width, axis=dim)
        before = lax.ppermute(last, axis, up)
        after = lax.ppermute(first, axis, down)
        x = jnp.concatenate([before, x, after], axis=dim)
    return x


def silu_slope(preact):
    sigma = jax.nn.sigmoid(preact)
    return sigma * (1.0 + preact * (1.0 - sigma))


def exact(left_side, right_side):
    return jnp.dot(left_side, right_side, precision=HIGH, preferred_element_type=jnp.float32)


def packed_side(leading, vectors, places, row_list):
    return jnp.concatenate(
        [
            leading[row_list].astype(jnp.float32),
            vectors[row_list].astype(jnp.float32),
            places[:, row_list].T,
        ],
        axis=1,
    )


def outgoing_rows(payload, row_lists):
    leading, vectors, places = payload
    return jnp.stack(
        [
            packed_side(leading, vectors, places, row_lists[0]),
            packed_side(leading, vectors, places, row_lists[1]),
        ]
    )


def split_side(packed, lead_width, vec_width):
    return (
        packed[:, :lead_width],
        packed[:, lead_width : lead_width + vec_width],
        packed[:, lead_width + vec_width :].T,
    )


def append_rows(payload, arrived, axis_number, cell_length):
    leading, vectors, places = payload
    lead_width = leading.shape[1]
    vec_width = vectors.shape[1]
    below = split_side(arrived[0], lead_width, vec_width)
    above = split_side(arrived[3], lead_width, vec_width)
    lift = jnp.where(jnp.arange(3) == axis_number, cell_length, 0.0).astype(jnp.float32)[:, None]
    leading = jnp.concatenate(
        [leading, below[0].astype(jnp.bfloat16), above[0].astype(jnp.bfloat16)], axis=0
    )
    vectors = jnp.concatenate(
        [vectors, below[1].astype(jnp.bfloat16), above[1].astype(jnp.bfloat16)], axis=0
    )
    places = jnp.concatenate([places, below[2] - lift, above[2] + lift], axis=1)
    return (leading, vectors, places)


def returned_rows(gradients, start_row, rows_each):
    leading, vectors, places = gradients
    upper = start_row + rows_each
    ending = start_row + 2 * rows_each
    lower_side = jnp.concatenate(
        [leading[start_row:upper], vectors[start_row:upper], places[:, start_row:upper].T], axis=1
    )
    upper_side = jnp.concatenate(
        [leading[upper:ending], vectors[upper:ending], places[:, upper:ending].T], axis=1
    )
    return jnp.stack([lower_side, upper_side])


def absorb_rows(gradients, start_row, arrived, row_lists):
    leading, vectors, places = gradients
    lead_width = leading.shape[1]
    vec_width = vectors.shape[1]
    below = split_side(arrived[0], lead_width, vec_width)
    above = split_side(arrived[3], lead_width, vec_width)
    leading = leading[:start_row].at[row_lists[0]].add(below[0]).at[row_lists[1]].add(above[0])
    vectors = vectors[:start_row].at[row_lists[0]].add(below[1]).at[row_lists[1]].add(above[1])
    places = (
        places[:, :start_row].at[:, row_lists[0]].add(below[2]).at[:, row_lists[1]].add(above[2])
    )
    return (leading, vectors, places)


def local(
    scalar_feat,
    vector_feat,
    positions,
    message_inner,
    message_inner_bias,
    message_outer,
    message_outer_bias,
    radial_weight,
    radial_bias,
    update_left,
    update_right,
    update_inner,
    update_inner_bias,
    update_outer,
    update_outer_bias,
    scalar_cotangent,
    vector_cotangent,
    x_face_rows,
    y_face_rows,
    z_face_rows,
    neighbour_table,
    hub_atoms,
    hub_table,
    hub_count,
):
    owned_count, feat_width = scalar_feat.shape
    cell_length = G * SPACING
    rows_x = x_face_rows.shape[2]
    rows_y = y_face_rows.shape[2]
    rows_z = z_face_rows.shape[2]
    start_y = owned_count + 2 * rows_x
    start_z = start_y + 2 * rows_y
    payload = (scalar_feat, vector_feat, positions)
    arrived = with_halo(outgoing_rows(payload, x_face_rows[0]), (("gx", 0),), 1)
    payload = append_rows(payload, arrived, 0, cell_length)
    arrived = with_halo(outgoing_rows(payload, y_face_rows[0]), (("gy", 0),), 1)
    payload = append_rows(payload, arrived, 1, cell_length)
    arrived = with_halo(outgoing_rows(payload, z_face_rows[0]), (("gz", 0),), 1)
    ext_leading, ext_vectors, ext_places = append_rows(payload, arrived, 2, cell_length)
    preact = (
        jnp.dot(ext_leading, message_inner, preferred_element_type=jnp.float32) + message_inner_bias
    )
    hidden = jax.nn.silu(preact).astype(jnp.bfloat16)
    filters = (
        jnp.dot(hidden, message_outer, preferred_element_type=jnp.float32) + message_outer_bias
    ).astype(jnp.bfloat16)
    ext_rows = ext_places.shape[1]
    orders = jnp.arange(1, radial_weight.shape[0] + 1, dtype=jnp.float32)[:, None]
    radial_wide = radial_weight.astype(jnp.float32)

    def edge_state(source, target):
        offset = jnp.take(ext_places, source, axis=1) - jnp.take(ext_places, target, axis=1)
        distance = jnp.sqrt(jnp.sum(offset * offset, axis=0))
        direction = offset / distance
        phase_arg = orders * (math.pi / CUTOFF) * distance[None, :]
        radial_basis = (jnp.sin(phase_arg) / distance[None, :]).astype(jnp.bfloat16)
        inside = distance < CUTOFF
        cutoff_factor = jnp.where(inside, 0.5 * (jnp.cos(math.pi / CUTOFF * distance) + 1.0), 0.0)
        linear = (
            jnp.einsum("kn,kc->nc", radial_basis, radial_weight, preferred_element_type=jnp.float32)
            + radial_bias
        )
        edge_filter = linear * cutoff_factor[:, None]
        neighbour_filters = jnp.take(filters, source, axis=0)
        neighbour_vectors = jnp.take(ext_vectors, source, axis=0).reshape(-1, 3, feat_width)
        mixture = neighbour_filters * edge_filter
        return (
            distance,
            direction,
            phase_arg,
            radial_basis,
            inside,
            cutoff_factor,
            linear,
            edge_filter,
            neighbour_filters,
            neighbour_vectors,
            mixture,
        )

    def message_terms(source, target, weight):
        state = edge_state(source, target)
        direction = state[1]
        neighbour_vectors = state[9]
        mixture = state[10] * weight
        scalar_part = mixture[:, feat_width : 2 * feat_width]
        vector_part = (
            neighbour_vectors * mixture[:, None, :feat_width]
            + mixture[:, None, 2 * feat_width :] * direction.T[:, :, None]
        )
        return (scalar_part, vector_part.reshape(-1, 3 * feat_width))

    regular_weight = jnp.ones((owned_count, 1), jnp.float32)
    targets = jnp.arange(owned_count, dtype=jnp.int32)
    hub_slots = hub_atoms.shape[0]
    live_weight = (jnp.arange(hub_slots) < hub_count[0]).astype(jnp.float32)[:, None]

    def regular_forward(totals, source):
        scalar_part, vector_part = message_terms(source, targets, regular_weight)
        return ((totals[0] + scalar_part, totals[1] + vector_part), None)

    def hub_forward(totals, source):
        scalar_part, vector_part = message_terms(source, hub_atoms, live_weight)
        return ((totals[0] + scalar_part, totals[1] + vector_part), None)

    delta_scalar, delta_vector = lax.scan(
        regular_forward,
        (
            jnp.zeros((owned_count, feat_width), jnp.float32),
            jnp.zeros((owned_count, 3 * feat_width), jnp.float32),
        ),
        neighbour_table,
    )[0]
    hub_scalar, hub_vector = lax.scan(
        hub_forward,
        (
            jnp.zeros((hub_slots, feat_width), jnp.float32),
            jnp.zeros((hub_slots, 3 * feat_width), jnp.float32),
        ),
        hub_table,
    )[0]
    delta_scalar = delta_scalar.at[hub_atoms].add(hub_scalar)
    delta_vector = delta_vector.at[hub_atoms].add(hub_vector)
    state_s = scalar_feat.astype(jnp.float32) + delta_scalar
    state_v = vector_feat.astype(jnp.float32) + delta_vector
    low_vector = state_v.astype(jnp.bfloat16).reshape(owned_count, 3, feat_width)
    left_part = jnp.einsum(
        "acf,fg->acg", low_vector, update_left, preferred_element_type=jnp.float32
    )
    right_part = jnp.einsum(
        "acf,fg->acg", low_vector, update_right, preferred_element_type=jnp.float32
    )
    inner_part = jnp.sum(left_part * right_part, axis=1)
    norm_part = jnp.sqrt(jnp.sum(right_part * right_part, axis=1) + 1.0)
    joined = jnp.concatenate([state_s, norm_part], axis=1).astype(jnp.bfloat16)
    preact_up = (
        jnp.dot(joined, update_inner, preferred_element_type=jnp.float32) + update_inner_bias
    )
    hidden_up = jax.nn.silu(preact_up).astype(jnp.bfloat16)
    amplitude = (
        jnp.dot(hidden_up, update_outer, preferred_element_type=jnp.float32) + update_outer_bias
    )
    amp_vv = amplitude[:, :feat_width]
    amp_sv = amplitude[:, feat_width : 2 * feat_width]
    amp_ss = amplitude[:, 2 * feat_width :]
    out_scalar = state_s + amp_sv * inner_part + amp_ss
    out_vector = state_v + (amp_vv[:, None, :] * left_part).reshape(owned_count, 3 * feat_width)
    cot_scalar = scalar_cotangent.astype(jnp.float32)
    cot_vector = vector_cotangent.astype(jnp.float32).reshape(owned_count, 3, feat_width)
    grad_amplitude = jnp.concatenate(
        [jnp.sum(cot_vector * left_part, axis=1), cot_scalar * inner_part, cot_scalar], axis=1
    )
    grad_left = cot_vector * amp_vv[:, None, :] + (cot_scalar * amp_sv)[:, None, :] * right_part
    grad_right = (cot_scalar * amp_sv)[:, None, :] * left_part
    update_outer_grad = exact(hidden_up.astype(jnp.float32).T, grad_amplitude)
    update_outer_bias_grad = jnp.sum(grad_amplitude, axis=0)
    grad_preact_up = exact(grad_amplitude, update_outer.astype(jnp.float32).T) * silu_slope(
        preact_up
    )
    update_inner_grad = exact(joined.astype(jnp.float32).T, grad_preact_up)
    update_inner_bias_grad = jnp.sum(grad_preact_up, axis=0)
    grad_joined = exact(grad_preact_up, update_inner.astype(jnp.float32).T)
    grad_right = grad_right + (grad_joined[:, feat_width:] / norm_part)[:, None, :] * right_part
    low_wide = low_vector.astype(jnp.float32)
    update_left_grad = jnp.einsum("acf,acg->fg", low_wide, grad_left, precision=HIGH)
    update_right_grad = jnp.einsum("acf,acg->fg", low_wide, grad_right, precision=HIGH)
    grad_state_v = (
        cot_vector
        + jnp.einsum("acg,fg->acf", grad_left, update_left.astype(jnp.float32), precision=HIGH)
        + jnp.einsum("acg,fg->acf", grad_right, update_right.astype(jnp.float32), precision=HIGH)
    ).reshape(owned_count, 3 * feat_width)
    grad_state_s = cot_scalar + grad_joined[:, :feat_width]

    def edge_backward(source, target, weight, carry):
        grad_filters, grad_vectors, grad_places, grad_radial, grad_radial_bias = carry
        (
            distance,
            direction,
            phase_arg,
            radial_basis,
            inside,
            cutoff_factor,
            linear,
            edge_filter,
            neighbour_filters,
            neighbour_vectors,
            mixture,
        ) = edge_state(source, target)
        grad_scalar_edge = jnp.take(grad_state_s, target, axis=0) * weight
        grad_vector_edge = (
            jnp.take(grad_state_v, target, axis=0).reshape(-1, 3, feat_width) * weight[:, :, None]
        )
        grad_mixture = jnp.concatenate(
            [
                jnp.sum(grad_vector_edge * neighbour_vectors, axis=1),
                grad_scalar_edge,
                jnp.sum(grad_vector_edge * direction.T[:, :, None], axis=1),
            ],
            axis=1,
        )
        grad_neighbour_vec = (grad_vector_edge * mixture[:, None, :feat_width]).reshape(
            -1, 3 * feat_width
        )
        grad_direction = jnp.sum(grad_vector_edge * mixture[:, None, 2 * feat_width :], axis=2).T
        grad_filter = grad_mixture * neighbour_filters
        grad_cutoff = jnp.sum(grad_filter * linear, axis=1)
        grad_linear = grad_filter * cutoff_factor[:, None]
        grad_radial = grad_radial + jnp.einsum(
            "kn,nc->kc", radial_basis.astype(jnp.float32), grad_linear, precision=HIGH
        )
        grad_radial_bias = grad_radial_bias + jnp.sum(grad_linear, axis=0)
        grad_basis = jnp.einsum("nc,kc->kn", grad_linear, radial_wide, precision=HIGH)
        basis_slope = (
            orders * (math.pi / CUTOFF) * jnp.cos(phase_arg)
            - jnp.sin(phase_arg) / distance[None, :]
        ) / distance[None, :]
        cutoff_slope = jnp.where(
            inside, -0.5 * (math.pi / CUTOFF) * jnp.sin(math.pi / CUTOFF * distance), 0.0
        )
        grad_distance = jnp.sum(grad_basis * basis_slope, axis=0) + grad_cutoff * cutoff_slope
        grad_offset = (
            grad_direction - direction * jnp.sum(direction * grad_direction, axis=0)
        ) / distance + grad_distance * direction
        grad_filters = grad_filters.at[source].add(grad_mixture * edge_filter)
        grad_vectors = grad_vectors.at[source].add(grad_neighbour_vec)
        grad_places = grad_places.at[:, source].add(grad_offset).at[:, target].add(-grad_offset)
        return (grad_filters, grad_vectors, grad_places, grad_radial, grad_radial_bias)

    def regular_backward(carry, source):
        return (edge_backward(source, targets, regular_weight, carry), None)

    def hub_backward(carry, source):
        return (edge_backward(source, hub_atoms, live_weight, carry), None)

    carry = (
        jnp.zeros((ext_rows, 3 * feat_width), jnp.float32),
        jnp.zeros((ext_rows, 3 * feat_width), jnp.float32),
        jnp.zeros((3, ext_rows), jnp.float32),
        jnp.zeros(radial_weight.shape, jnp.float32),
        jnp.zeros((3 * feat_width,), jnp.float32),
    )
    carry = lax.scan(regular_backward, carry, neighbour_table)[0]
    carry = lax.scan(hub_backward, carry, hub_table)[0]
    grad_filters, grad_vectors, grad_places, radial_weight_grad, radial_bias_grad = carry
    grad_vectors = grad_vectors.at[:owned_count].add(grad_state_v)
    grad_preact = exact(grad_filters, message_outer.astype(jnp.float32).T) * silu_slope(preact)
    message_outer_grad = exact(hidden.astype(jnp.float32).T, grad_filters)
    message_outer_bias_grad = jnp.sum(grad_filters, axis=0)
    message_inner_grad = exact(ext_leading.astype(jnp.float32).T, grad_preact)
    message_inner_bias_grad = jnp.sum(grad_preact, axis=0)
    grad_leading = (
        exact(grad_preact, message_inner.astype(jnp.float32).T).at[:owned_count].add(grad_state_s)
    )
    gradients = (grad_leading, grad_vectors, grad_places)
    arrived = with_halo(returned_rows(gradients, start_z, rows_z), (("gz", 0),), 1)
    gradients = absorb_rows(gradients, start_z, arrived, z_face_rows[0])
    arrived = with_halo(returned_rows(gradients, start_y, rows_y), (("gy", 0),), 1)
    gradients = absorb_rows(gradients, start_y, arrived, y_face_rows[0])
    arrived = with_halo(returned_rows(gradients, owned_count, rows_x), (("gx", 0),), 1)
    gradients = absorb_rows(gradients, owned_count, arrived, x_face_rows[0])
    scalar_grad = gradients[0]
    summed = lax.psum(
        (
            message_inner_grad,
            message_inner_bias_grad,
            message_outer_grad,
            message_outer_bias_grad,
            radial_weight_grad,
            radial_bias_grad,
            update_left_grad,
            update_right_grad,
            update_inner_grad,
            update_inner_bias_grad,
            update_outer_grad,
            update_outer_bias_grad,
        ),
        ("gx", "gy", "gz"),
    )
    return (
        out_scalar.astype(jnp.bfloat16),
        out_vector.astype(jnp.bfloat16),
        scalar_grad,
        gradients[1],
        gradients[2],
        summed[0],
        summed[1],
        summed[2],
        summed[3],
        summed[4],
        summed[5],
        summed[6],
        summed[7],
        summed[8],
        summed[9],
        summed[10],
        summed[11],
    )


def solution(mesh):
    return jax.shard_map(
        local,
        mesh=mesh,
        in_specs=(
            P(("gx", "gy", "gz"), None),
            P(("gx", "gy", "gz"), None),
            P(None, ("gx", "gy", "gz")),
            P(),
            P(),
            P(),
            P(),
            P(),
            P(),
            P(),
            P(),
            P(),
            P(),
            P(),
            P(),
            P(("gx", "gy", "gz"), None),
            P(("gx", "gy", "gz"), None),
            P(("gx", "gy", "gz"), None, None),
            P(("gx", "gy", "gz"), None, None),
            P(("gx", "gy", "gz"), None, None),
            P(None, ("gx", "gy", "gz")),
            P(("gx", "gy", "gz")),
            P(None, ("gx", "gy", "gz")),
            P(("gx", "gy", "gz")),
        ),
        out_specs=(
            P(("gx", "gy", "gz"), None),
            P(("gx", "gy", "gz"), None),
            P(("gx", "gy", "gz"), None),
            P(("gx", "gy", "gz"), None),
            P(None, ("gx", "gy", "gz")),
            P(),
            P(),
            P(),
            P(),
            P(),
            P(),
            P(),
            P(),
            P(),
            P(),
            P(),
            P(),
        ),
        check_vma=False,
    )
```

profile of v0, /device:TPU:1, one launch (start us, length us, event | category | flops | bytes accessed | tf_op | source)
XLA Modules:
  0.0 3244.8 jit_solution(17040707537111359966)
XLA Ops:
  104.8 105.9 %while.80 = (s32[]{:T(128)}, f32[128,128]{1,0:T(8,128)}, f32[128,384]{1,0:T(8,128)}, s32[11,128]{1,0:T(8,128)}, bf16[1728,384]{1,0:T(8,128)(2,1)S(1)}, /*index=5...) while((s32[]{:T(128)}, f32[128,128]{1,0:T(8,128)}, ...), condition=%wide.region_5.10_spmd.clone, body=%wide.region_3.0_spmd.clone.sunk | while | flops 2650795 | bytes 4173808 | solution.py:225
  211.9 659.4 %while.79 = (s32[]{:T(128)}, f32[1000,128]{1,0:T(8,128)}, f32[1000,384]{1,0:T(8,128)}, s32[15,1000]{1,0:T(8,128)}, bf16[1728,384]{1,0:T(8,128)(2,1)S(1)}, /*inde...) while((s32[]{:T(128)}, f32[1000,128]{1,0:T(8,128)}, ...), condition=%wide.region_2.5_spmd.clone, body=%wide.region_0.4_spmd.clone.sunk | while | flops 20319064 | bytes 32466348 | solution.py:217
  943.9 1611.9 %while.81 = (s32[]{:T(128)}, f32[1728,384]{1,0:T(8,128)}, f32[1728,384]{1,0:T(8,128)}, f32[3,1728]{0,1:T(8,128)}, f32[20,384]{1,0:T(8,128)}, /*index=5*/f32[384]...) while((s32[]{:T(128)}, f32[1728,384]{1,0:T(8,128)}, ...), condition=%wide.region_24.29_spmd.clone.clone, body=%wide.region_11.28_spmd.clone.clone.sunk | while | flops 212583808 | bytes 57641116 | solution.py:353
  998.7 11.2 scatter_custom_fusion.81
  1016.9 9.2 scatter_custom_fusion.83
  1026.0 8.8 scatter_custom_fusion.84
  1041.0 10.4 scatter_fusion
  1106.1 11.2 scatter_custom_fusion.81
  1124.3 9.2 scatter_custom_fusion.83
  1133.4 8.8 scatter_custom_fusion.84
  1148.4 10.4 scatter_fusion
  1213.5 11.2 scatter_custom_fusion.81
  1231.7 9.2 scatter_custom_fusion.83
  1240.9 8.8 scatter_custom_fusion.84
  1255.9 10.4 scatter_fusion
  1320.9 11.2 scatter_custom_fusion.81
  1339.1 9.2 scatter_custom_fusion.83
  1348.3 8.8 scatter_custom_fusion.84
  1363.3 10.4 scatter_fusion
  1428.4 11.2 scatter_custom_fusion.81
  1446.6 9.2 scatter_custom_fusion.83
  1455.7 8.8 scatter_custom_fusion.84
  1470.7 10.4 scatter_fusion
  1535.8 11.2 scatter_custom_fusion.81
  1554.0 9.2 scatter_custom_fusion.83
  1563.1 8.8 scatter_custom_fusion.84
  1578.1 10.4 scatter_fusion
  1643.2 11.2 scatter_custom_fusion.81
  1661.4 9.2 scatter_custom_fusion.83
  1670.6 8.8 scatter_custom_fusion.84
  1685.6 10.4 scatter_fusion
  1750.6 11.2 scatter_custom_fusion.81
  1768.8 9.2 scatter_custom_fusion.83
  1778.0 8.8 scatter_custom_fusion.84
  1793.0 10.4 scatter_fusion
  1858.1 11.2 scatter_custom_fusion.81
  1876.3 9.2 scatter_custom_fusion.83
  1885.4 8.8 scatter_custom_fusion.84
  1900.4 10.4 scatter_fusion
  1965.5 11.2 scatter_custom_fusion.81
  1983.7 9.2 scatter_custom_fusion.83
  2007.8 10.4 scatter_fusion
  2072.9 11.2 scatter_custom_fusion.81
  2091.1 9.2 scatter_custom_fusion.83
  2100.3 8.8 scatter_custom_fusion.84
  2115.3 10.4 scatter_fusion
  2180.3 11.2 scatter_custom_fusion.81
  2198.5 9.2 scatter_custom_fusion.83
  2222.7 10.4 scatter_fusion
  2287.8 11.2 scatter_custom_fusion.81
  2306.0 9.2 scatter_custom_fusion.83
  2315.1 8.8 scatter_custom_fusion.84
  2330.1 10.4 scatter_fusion
  2395.2 11.2 scatter_custom_fusion.81
  2413.4 9.2 scatter_custom_fusion.83
  2422.5 8.8 scatter_custom_fusion.84
  2437.5 10.4 scatter_fusion
  2502.6 11.2 scatter_custom_fusion.81
  2520.8 9.2 scatter_custom_fusion.83
  2530.0 8.8 scatter_custom_fusion.84
  2545.0 10.4 scatter_fusion
  2555.8 476.0 %while.82 = (s32[]{:T(128)}, f32[1728,384]{1,0:T(8,128)}, f32[1728,384]{1,0:T(8,128)}, f32[3,1728]{0,1:T(8,128)}, f32[20,384]{1,0:T(8,128)}, /*index=5*/f32[384]...) while((s32[]{:T(128)}, f32[1728,384]{1,0:T(8,128)}, ...), condition=%wide.region_38.43_spmd.clone.clone.clone, body=%wide.region_25.42_spmd.clone.clone.clone.sunk | while | flops 27824680 | bytes 10331057 | solution.py:354
  3092.7 46.5 %all-reduce = (f32[128]{0:T(128)}, f32[384]{0:T(512)}, f32[20,384]{1,0:T(8,128)}, f32[384]{0:T(512)}, f32[128]{0:T(128)}, /*index=5*/f32[384]{0:T(512)}) all-reduce(f32[128]{0:T(128)S(1)} %get-tuple-element.1687, f32[384]{0:T(512)S(1)} %reduce_sum.281, ...), channel_id=1, replica_groups=mesh['gx'=2,'gy'=4,'gz'=4] {'gx','gy','gz'}, use_global_device_ids=true, to_apply=%region_59.64 | all-reduce | flops 9088 | bytes 72704 | tf_op jit(solution)/shard_map/psum | solution.py:373
  3186.3 42.2 %all-reduce.4.cloned.1.call-done = (f32[128,128]{1,0:T(8,128)}, f32[128,384]{1,0:T(8,128)}, f32[128,128]{1,0:T(8,128)}, f32[128,128]{1,0:T(8,128)}, f32[256,128]{1,0:T(8,128)}, /*index=5*/f32[128,384]{1,0:T(8,128)}) async-done(((f32[128,128]{1,0:T(8,128)}, f32[128,384]{1,0:T(8,128)}, f32[128,128]{1,0:T(8,128)}, f32[128,128]{1,0:T(8,128)}, f32[256,128]{1,0:T(8,128)}, /*index=5*/f32[128,384]{1,0:T(8,128)}), ...) | async-done | bytes 720912 | tf_op jit(solution)/shard_map/psum | solution.py:373
  (2690 shorter events, 2558.0 us)
Async XLA Ops:
  7.2 96.7 %copy-start = (bf16[128,384]{1,0:T(8,128)(2,1)S(1)}, bf16[128,384]{1,0:T(8,128)(2,1)}, u32[]{:S(2)}) copy-start(bf16[128,384]{1,0:T(8,128)(2,1)} %param.49) | copy-start | bytes 294916
  7.2 3221.3 %all-reduce.4.cloned.1.call-start = ((), (), s32[]{:S(2)}) async-start(), calls=%async_computation | async-start | bytes 1441792 | tf_op jit(solution)/shard_map/psum | solution.py:373
  13.4 8.5 collective-permute-start
  17.7 9.7 collective-permute-start.1
  21.9 30.9 copy-start.85
  22.0 36.6 %copy-start.63 = (bf16[100,384]{1,0:T(8,128)(2,1)}, bf16[100,384]{1,0:T(8,128)(2,1)S(1)}, u32[]{:S(2)}) copy-start(bf16[100,384]{1,0:T(8,128)(2,1)S(1)} %slice.526) | copy-start | bytes 230404
  27.4 31.2 copy-start.64
  36.0 15.0 collective-permute-start.3
  43.6 8.4 collective-permute-start.2
  64.7 12.1 collective-permute-start.5
  72.1 15.3 copy-start.80
  72.1 15.3 copy-start.82
  72.1 13.0 collective-permute-start.4
  79.1 13.8 copy-start.136
  79.1 14.5 copy-start.86
  79.1 14.5 copy-start.89
  88.1 14.7 copy-start.30
  104.8 105.9 %copy-start.132 = (pred[1000]{0:T(1024)(128)(4,1)S(1)}, pred[1000]{0:T(1024)(128)(4,1)}, u32[]{:S(2)}) copy-start(pred[1000]{0:T(1024)(128)(4,1)} %broadcast_compare_fusion.1) | copy-start | bytes 3004
  2555.8 12.2 copy-start.42
  2555.8 12.2 copy-start.102
  2556.5 13.4 copy-start.111
  2562.8 13.7 copy-start.103
  2562.8 13.7 copy-start.114
  2599.8 13.4 copy-start.111
  2606.0 13.7 copy-start.103
  2606.0 13.7 copy-start.114
  2643.0 13.4 copy-start.111
  2649.3 13.7 copy-start.103
  2649.3 13.7 copy-start.114
  2686.3 13.4 copy-start.111
  2692.6 13.7 copy-start.103
  2692.6 13.7 copy-start.114
  2729.6 13.4 copy-start.111
  2735.8 13.7 copy-start.103
  2735.8 13.7 copy-start.114
  2772.2 12.2 copy-start.102
  2772.9 13.4 copy-start.111
  2779.1 13.7 copy-start.103
  2779.1 13.7 copy-start.114
  2816.1 13.4 copy-start.111
  2822.4 13.7 copy-start.103
  2822.4 13.7 copy-start.114
  2859.4 13.4 copy-start.111
  2865.6 13.7 copy-start.103
  2865.6 13.7 copy-start.114
  2902.7 13.4 copy-start.111
  2908.9 13.7 copy-start.103
  2908.9 13.7 copy-start.114
  2945.9 13.4 copy-start.111
  2952.2 13.7 copy-start.103
  2952.2 13.7 copy-start.114
  2989.2 13.4 copy-start.111
  2995.4 13.7 copy-start.103
  2995.4 13.7 copy-start.114
  3053.3 11.7 collective-permute-start.6
  3056.4 19.7 collective-permute-start.7
  3086.7 56.8 %collective-permute-start.8 = (f32[1,120,515]{2,1,0:T(8,128)}, f32[1,120,515]{2,1,0:T(8,128)}, u32[]{:S(2)}, u32[]{:S(2)}) collective-permute-start(f32[1,120,515]{2,1,0:T(8,128)} %maximum_bitcast_fusion.6), channel_id=1, source_target_pairs={{0,4},{4,8},{8,12},{12,0},{1,5},{5,9},{9,13},{13,1},{2,6},{6,10},{... | collective-permute-start | bytes 741608 | tf_op jit(solution)/shard_map/ppermute | solution.py:23
  3090.1 62.9 %collective-permute-start.9 = (f32[1,120,515]{2,1,0:T(8,128)}, f32[1,120,515]{2,1,0:T(8,128)}, u32[]{:S(2)}, u32[]{:S(2)}) collective-permute-start(f32[1,120,515]{2,1,0:T(8,128)} %maximum_bitcast_fusion.7), channel_id=1, source_target_pairs={{4,0},{8,4},{12,8},{0,12},{5,1},{9,5},{13,9},{1,13},{6,2},{10,6},{... | collective-permute-start | bytes 741608 | tf_op jit(solution)/shard_map/ppermute | solution.py:24
  3092.7 49.4 %copy-start.24 = (f32[1440,384]{1,0:T(8,128)S(1)}, f32[1440,384]{1,0:T(8,128)}, u32[]{:S(2)}) copy-start(f32[1440,384]{1,0:T(8,128)} %scatter_custom_fusion.13) | copy-start | bytes 6635524
  3156.5 13.2 copy-start.33
  3167.5 7.3 collective-permute-start.10
  3168.6 12.2 collective-permute-start.11
  3184.8 52.9 %copy-start.58 = (f32[1000,384]{1,0:T(8,128)}, f32[1000,384]{1,0:T(8,128)S(1)}, u32[]{:S(2)}) copy-start(f32[1000,384]{1,0:T(8,128)S(1)} %scatter_custom_fusion.25) | copy-start | bytes 4608004
  3186.3 51.5 %copy-start.83 = (f32[1000,128]{1,0:T(8,128)}, f32[1000,128]{1,0:T(8,128)S(1)}, u32[]{:S(2)}) copy-start(f32[1000,128]{1,0:T(8,128)S(1)} %scatter_custom_fusion.23) | copy-start | bytes 1536004
  (470 other events, 2807.6 us)
Sparse Core Ops, SparseCore 0:
  3091.6 136.8 all-reduce.3
where the time goes:
time: 3290 us; the launch traced here: 3240 us
  other arithmetic  1600 us (49%)
  local copies, waits for them, and re-layouts  1290 us (39%)
  matrix products  215 us (7%)
  waiting for transfers between devices  63.6 us (2%)
  blocking collectives  46.5 us (1%)
    scatter-add x52, other arithmetic, edge_backward(): grad_places.at[:, source].add(grad_offset).at[:, target].add(-grad_offset)  345 us
    scatter-add x26, other arithmetic, edge_backward(): grad_filters = grad_filters.at[source].add(grad_mixture * edge_filter)  222 us
    scatter-add x26, other arithmetic, edge_backward(): grad_vectors = grad_vectors.at[source].add(grad_neighbour_vec)  207 us
    gather x52, local copies, waits for them, and re-layouts, edge_state(): jnp.take(ext_places, source, axis=1) - jnp.take(ext_places, target, axis=1)  196 us
    gather x52, local copies, waits for them, and re-layouts, edge_state(): jnp.take(ext_vectors, source, axis=0).reshape(-1, 3, feat_width)  180 us
    gather x52, local copies, waits for them, and re-layouts, edge_state(): neighbour_filters = jnp.take(filters, source, axis=0)  173 us
    dot_general x52, matrix products, edge_state(): jnp.einsum('kn,kc->nc', radial_basis, radial_weight, preferred_element_ty...  85.4 us
    mul x52, local copies, waits for them, and re-layouts, message_terms(): neighbour_vectors * mixture[:, None, :feat_width]  84.1 us
  transfers between devices with their start and end apart: 13, of which 6 were waited for; matrix products, arithmetic and copies ran while one was open for 3% of the time, Pallas kernels for 0%

commit v1 on v0

v1 whole, which is shorter than its diff:
```python
import functools
import math

import jax
import jax.numpy as jnp
from jax import lax
from jax.experimental import pallas as pl
from jax.experimental.pallas import tpu as pltpu
from jax.sharding import PartitionSpec as P

G = 10
SPACING = 2.6
CUTOFF = 5.0

LANES = 128
TILE = 8
STEP = 9
SLOTS = 16
ORDER_ROWS = 24
GROUP = 3
PARTS = 4
MIB = 1024 * 1024
f32 = jnp.float32
bf16 = jnp.bfloat16

NN = ((1,), (0,))
NT = ((1,), (1,))
TN = ((0,), (0,))


def up_to(count, step):
    return -(-count // step) * step


def mm(left_side, right_side, dims=NN):
    return lax.dot_general(
        left_side, right_side, (dims, ((), ())), preferred_element_type=f32
    )


def halves(x):
    high = x.astype(bf16)
    return high, (x - high.astype(f32)).astype(bf16)


def thirds(x):
    high = x.astype(bf16)
    rest = x - high.astype(f32)
    middle = rest.astype(bf16)
    return high, middle, (rest - middle.astype(f32)).astype(bf16)


def pick_exact(values, onehot):
    stacked = jnp.concatenate([x.astype(f32) for x in thirds(values)], axis=0).astype(bf16)
    moved = mm(stacked, onehot, NT)
    return (moved[0:TILE] + moved[TILE : 2 * TILE]) + moved[2 * TILE :]


def packed_rows(count):
    return up_to(count + -(-count // LANES), TILE)


def iota(shape, dim):
    return lax.broadcasted_iota(jnp.int32, shape, dim)


def read_places(ref, count):
    pieces = []
    sub = iota((TILE, LANES), 0)
    for part in range(-(-count // LANES)):
        row = count + part
        rows = [
            jnp.broadcast_to(ref[row : row + 1, c * LANES : (c + 1) * LANES], (TILE, LANES))
            for c in range(3)
        ]
        pieces.append(
            jnp.where(sub == 0, rows[0], jnp.where(sub == 1, rows[1], jnp.where(sub == 2, rows[2], 0.0)))
        )
    return pieces[0] if len(pieces) == 1 else jnp.concatenate(pieces, axis=1)


def write_places(ref, count, places):
    width = places.shape[1]
    for part in range(-(-count // LANES)):
        size = min(LANES, width - part * LANES)
        for c in range(3):
            ref[count + part : count + part + 1, c * LANES : c * LANES + size] = places[
                c : c + 1, part * LANES : part * LANES + size
            ]


def shifted_places(ref, count, axis_number, amount):
    places = read_places(ref, count)
    sub = iota(places.shape, 0)
    return places + jnp.where(sub == axis_number, amount, 0.0)


def pair_views(refs, rows):
    if len(refs) == 2:
        return list(refs)
    return [refs[0].at[pl.ds(0, rows)], refs[0].at[pl.ds(rows, rows)]]


def arrived_views(counts, shapes, refs):
    views = []
    at = 0
    for count, size in zip(counts, shapes):
        pair = pair_views(refs[at : at + size], packed_rows(count))
        views += pair if size == 2 else pair[::-1]
        at += size
    return views, refs[at:]


def pack_rows(halo, arrived, list_sc, rows, place, count, out_refs):
    owned = rows.shape[0]
    count8 = up_to(count, TILE)
    columns = list_sc[...].T
    for side, out_ref in enumerate(out_refs):
        column = columns[0:count8, side : side + 1]
        out_ref[...] = jnp.zeros(out_ref.shape, f32)
        onehot = (column == iota((count8, owned), 1).astype(f32)).astype(bf16)
        total = mm(onehot, rows)
        places = pick_exact(place, onehot)
        for (first, size, axis_number, amount), ref in zip(halo, arrived):
            size8 = up_to(size, TILE)
            lane = iota((count8, size8), 1)
            onehot = ((column == (lane + first).astype(f32)) & (lane < size)).astype(bf16)
            total = total + mm(onehot, ref[0:size8, :].astype(bf16))
            arrived_places = shifted_places(ref, size, axis_number, amount)
            places = places + pick_exact(arrived_places[:, 0:size8], onehot)
        out_ref[0:count8, :] = total
        write_places(out_ref, count, places)


def first_pack_kernel(out_size, x_hbm, y_hbm, z_hbm, s_hbm, v_hbm, p_hbm, *rest):
    outs = rest[:out_size]
    (
        rows_ref,
        place_ref,
        y_out,
        z_out,
        x_ref,
        s_ref,
        v_ref,
        p_ref,
        list_sc,
        sems,
    ) = rest[out_size:]
    pairs = (
        (x_hbm, x_ref),
        (s_hbm, s_ref),
        (v_hbm, v_ref),
        (p_hbm, p_ref),
        (y_hbm, y_out),
        (z_hbm, z_out),
    )
    copies = [pltpu.make_async_copy(a, b, sems.at[n]) for n, (a, b) in enumerate(pairs)]
    for copy in copies:
        copy.start()
    count = x_ref.shape[1]
    place_ref[...] = jnp.zeros(place_ref.shape, f32)
    list_sc[...] = jnp.full(list_sc.shape, -1.0, f32)
    for copy in copies:
        copy.wait()
    list_sc[0:2, 0:count] = x_ref[...].astype(f32)
    place_ref[0:3, :] = p_ref[...]
    rows = jnp.concatenate([s_ref[...], v_ref[...]], axis=1)
    out_refs = pair_views(outs, packed_rows(count))
    pack_rows((), (), list_sc, rows, place_ref[...], count, out_refs)
    rows_ref[...] = rows.astype(f32)


def list_to(list_sc, list_ref):
    list_sc[...] = jnp.full(list_sc.shape, -1.0, f32)
    list_sc[0:2, 0 : list_ref.shape[1]] = list_ref[...].astype(f32)


def pack_own_kernel(y_list, z_list, rows_ref, place_ref, *rest):
    outs, list_sc = rest[:4], rest[4]
    rows = rows_ref[...].astype(bf16)
    for n, list_ref in enumerate((y_list, z_list)):
        list_to(list_sc, list_ref)
        pair = outs[2 * n : 2 * n + 2]
        pack_rows((), (), list_sc, rows, place_ref[...], list_ref.shape[1], pair)


def pack_kernel(halo, shapes, out_size, list_ref, own_lower, own_upper, *rest):
    arrived, rest = arrived_views([h[1] for h in halo[::2]], shapes, rest)
    count = list_ref.shape[1]
    count8 = up_to(count, TILE)
    out_refs = pair_views(rest[:out_size], packed_rows(count))
    list_sc = rest[out_size]
    list_to(list_sc, list_ref)
    columns = list_sc[...].T
    sizes = [up_to(h[1], TILE) for h in halo]
    values = jnp.concatenate(
        [ref[0:size, :] for size, ref in zip(sizes, arrived)], axis=0
    ).astype(bf16)
    for side, (own_ref, out_ref) in enumerate(zip((own_lower, own_upper), out_refs)):
        column = columns[0:count8, side : side + 1]
        pieces = []
        places = read_places(own_ref, count)[:, 0:count8]
        for (first, size, axis_number, amount), size8, ref in zip(halo, sizes, arrived):
            lane = iota((count8, size8), 1)
            onehot = ((column == (lane + first).astype(f32)) & (lane < size)).astype(bf16)
            pieces.append(onehot)
            moved = shifted_places(ref, size, axis_number, amount)
            places = places + pick_exact(moved[:, 0:size8], onehot)
        out_ref[...] = own_ref[...]
        total = own_ref[0:count8, :]
        at = 0
        for size8, onehot in zip(sizes, pieces):
            total = total + mm(onehot, values[at : at + size8, :])
            at += size8
        out_ref[0:count8, :] = total
        write_places(out_ref, count, places)


def packet_shapes(axis, count, width, extra):
    rows = packed_rows(count)
    if lax.axis_size(axis) == 2:
        return [jax.ShapeDtypeStruct((2 * rows + extra, width), f32)]
    return [jax.ShapeDtypeStruct((rows + extra, width), f32)] * 2


def first_pack(axis, lists, s, v, p):
    owned, width = s.shape
    count = lists[0].shape[1]
    out = packet_shapes(axis, count, 4 * width, 0)
    far = pl.BlockSpec(memory_space=pltpu.HBM)
    inputs = [pltpu.with_memory_space_constraint(x, pltpu.HBM) for x in (*lists, s, v, p)]
    results = pl.pallas_call(
        functools.partial(first_pack_kernel, len(out)),
        in_specs=[far] * 6,
        out_shape=tuple(out)
        + (
            jax.ShapeDtypeStruct((owned, 4 * width), f32),
            jax.ShapeDtypeStruct((TILE, owned), f32),
        )
        + tuple(jax.ShapeDtypeStruct(x.shape, x.dtype) for x in lists[1:]),
        scratch_shapes=[
            pltpu.VMEM(lists[0].shape, lists[0].dtype),
            pltpu.VMEM(s.shape, s.dtype),
            pltpu.VMEM(v.shape, v.dtype),
            pltpu.VMEM(p.shape, p.dtype),
            pltpu.VMEM((TILE, up_to(count, LANES)), f32),
            pltpu.SemaphoreType.DMA((6,)),
        ],
        compiler_params=pltpu.CompilerParams(vmem_limit_bytes=14 * MIB),
        name="pack_first",
    )(*inputs)
    return list(results[: len(out)]), results[len(out) :]


def pack_own(lists, rows, place):
    shapes = []
    for list_ref in lists:
        shapes += [jax.ShapeDtypeStruct((packed_rows(list_ref.shape[1]), rows.shape[1]), f32)] * 2
    longest = max(list_ref.shape[1] for list_ref in lists)
    return pl.pallas_call(
        pack_own_kernel,
        out_shape=tuple(shapes),
        scratch_shapes=[pltpu.VMEM((TILE, up_to(longest, LANES)), f32)],
        compiler_params=pltpu.CompilerParams(vmem_limit_bytes=14 * MIB),
        name="pack_own",
    )(*lists, rows, place)


def pack_sides(axis, lists, own, halo, shapes, arrived):
    count = lists.shape[1]
    out = packet_shapes(axis, count, own[0].shape[1], 0)
    return pl.pallas_call(
        functools.partial(pack_kernel, tuple(halo), tuple(shapes), len(out)),
        out_shape=tuple(out),
        scratch_shapes=[pltpu.VMEM((TILE, up_to(count, LANES)), f32)],
        compiler_params=pltpu.CompilerParams(vmem_limit_bytes=14 * MIB),
        name="pack_rows",
    )(lists, *own, *arrived)


def build_places(place_sc, p_ref, owned, halo, arrived):
    place_sc[...] = jnp.zeros(place_sc.shape, f32)
    place_sc[:, 0:owned] = p_ref[...]
    for (first, rows, axis_number, amount), ref in zip(halo, arrived):
        places = shifted_places(ref, rows, axis_number, amount)
        place_sc[:, first : first + rows] = places[:, 0:rows]


def order_kernel(
    table_ref,
    hub_table_ref,
    place_ref,
    table_out,
    flat_out,
    hub_out,
    target_out,
    place_out,
    wide_sc,
    stack_sc,
    tall_sc,
):
    listed, owned = table_ref.shape
    slots = wide_sc.shape[1]
    wide_sc[...] = jnp.zeros(wide_sc.shape, jnp.int32)
    wide_sc[0:listed, 0:owned] = table_ref[...]
    lane = iota((1, slots), 1)
    worst = jnp.max(wide_sc[...].astype(f32), axis=0, keepdims=True)
    inner = (worst < owned) & (lane < owned)
    flag = inner.astype(f32)
    before = (iota((slots, slots), 0) <= iota((slots, slots), 1)).astype(bf16)
    count = mm(jnp.broadcast_to(flag, (TILE, slots)).astype(bf16), before)[0:1, :]
    total = count[:, slots - 1 : slots]
    index = lane.astype(f32)
    slot = jnp.where(inner, count - 1.0, total + index - count)
    moved = (iota((slots, slots), 0).astype(f32) == slot).astype(bf16)
    table = wide_sc[...]
    stack_sc[...] = jnp.zeros(stack_sc.shape, f32)
    stack_sc[0:SLOTS] = (table >> 8).astype(f32)
    stack_sc[SLOTS : 2 * SLOTS] = (table & 255).astype(f32)
    stack_sc[32:33] = (lane >> 8).astype(f32)
    stack_sc[33:34] = (lane & 255).astype(f32)
    for n, part in enumerate(thirds(place_ref[...])):
        at = 40 + n * TILE
        stack_sc[at : at + TILE, 0:owned] = part.astype(f32)
    turned = mm(stack_sc[...].astype(bf16), moved, NT)
    sorted_table = turned[0:SLOTS] * 256.0 + turned[SLOTS : 2 * SLOTS]
    table_out[...] = sorted_table.astype(jnp.int32)
    place_out[...] = (turned[40:48] + turned[48:56]) + turned[56:64]
    target = jnp.minimum(turned[32:33] * 256.0 + turned[33:34], owned - 1.0)
    for b in range(slots // LANES):
        part = target[:, b * LANES : (b + 1) * LANES]
        target_out[b : b + 1, :] = part.astype(jnp.int32) * TILE
    target_out[TILE:, :] = jnp.broadcast_to(total, (TILE, LANES)).astype(jnp.int32)

    def in_use_order(values, groups, out_ref):
        tall_sc[...] = jnp.zeros(tall_sc.shape, f32)
        for b in range(values.shape[1] // LANES):
            block = jnp.concatenate(
                [
                    values[:, b * LANES : (b + 1) * LANES],
                    jnp.zeros((LANES - values.shape[0], LANES), f32),
                ],
                axis=0,
            )
            tall_sc[b * LANES : (b + 1) * LANES, :] = block.T * 8.0
        rows = iota((LANES, LANES), 0)
        lanes = iota((LANES, LANES), 1)
        total = None
        for n in range(TILE):
            part = tall_sc[pl.ds(n, groups, TILE), :]
            high = jnp.floor(part * (1.0 / 256.0))
            low = part - high * 256.0
            place = (lanes == rows * TILE + n).astype(bf16)
            value = mm(high.astype(bf16), place) * 256.0 + mm(low.astype(bf16), place)
            total = value if total is None else total + value
        out_ref[...] = total.astype(jnp.int32)

    in_use_order(sorted_table, slots // TILE, flat_out)
    hubs = jnp.concatenate(
        [
            hub_table_ref[...].astype(f32),
            jnp.zeros((SLOTS - hub_table_ref.shape[0], LANES), f32),
        ],
        axis=0,
    )
    in_use_order(hubs, LANES // TILE, hub_out)


def order_atoms(table, hub_table, place):
    slots = up_to(table.shape[1], LANES)
    return pl.pallas_call(
        order_kernel,
        out_shape=(
            jax.ShapeDtypeStruct((SLOTS, slots), jnp.int32),
            jax.ShapeDtypeStruct((slots // TILE, LANES), jnp.int32),
            jax.ShapeDtypeStruct((LANES // TILE, LANES), jnp.int32),
            jax.ShapeDtypeStruct((2 * TILE, LANES), jnp.int32),
            jax.ShapeDtypeStruct((TILE, slots), f32),
        ),
        scratch_shapes=[
            pltpu.VMEM((SLOTS, slots), jnp.int32),
            pltpu.VMEM((64, slots), f32),
            pltpu.VMEM((slots, LANES), f32),
        ],
        compiler_params=pltpu.CompilerParams(vmem_limit_bytes=24 * MIB),
        name="order_atoms",
    )(table, hub_table, place)


def build_radial(wext32, wext, wr_ref, br_ref):
    width = wr_ref.shape[1] // 3
    orders = wr_ref.shape[0]
    wr = wr_ref[...].astype(f32)
    br = br_ref[...]
    bias_high = br.astype(bf16).astype(f32)
    bias_low = br - bias_high
    wext32[...] = jnp.zeros(wext32.shape, f32)
    for block, (row, column) in enumerate(
        ((0, 0), (0, 1), (1, 2), (2, 3), (3, 4))
    ):
        source = min(block, 2)
        at = row * ORDER_ROWS
        lanes = slice(column * width, (column + 1) * width)
        cols = slice(source * width, (source + 1) * width)
        wext32[at : at + orders, lanes] = wr[:, cols]
        wext32[at + orders : at + orders + 1, lanes] = bias_high[:, cols]
        wext32[at + orders + 1 : at + orders + 2, lanes] = bias_low[:, cols]
    wext[...] = wext32[...].astype(bf16)


def load_indices(idx_sc, tpos_sc, table_ref, target_ref):
    blocks = table_ref.shape[1] // LANES
    rows = idx_sc.shape[0]
    for b in range(blocks):
        at = b * SLOTS
        lanes = slice(b * LANES, (b + 1) * LANES)
        idx_sc[at : at + SLOTS, :] = table_ref[:, lanes]
        for c in range(3):
            tpos_sc[c * rows + at : c * rows + at + SLOTS, :] = jnp.broadcast_to(
                target_ref[c : c + 1, lanes], (SLOTS, LANES)
            )


def load_hubs(idx_sc, tpos_sc, hub_table_ref, hub_row_ref, place_sc, owned):
    rows = idx_sc.shape[0]
    at = rows - SLOTS
    idx_sc[at:, :] = jnp.zeros((SLOTS, LANES), jnp.int32)
    idx_sc[at : at + hub_table_ref.shape[0], :] = hub_table_ref[...]
    hub = jnp.broadcast_to(hub_row_ref[...], (TILE, LANES))
    lane = hub & (LANES - 1)
    chunk = hub >> 7
    total = jnp.zeros((TILE, LANES), f32)
    for t in range(-(-owned // LANES)):
        part = jnp.take_along_axis(
            place_sc[:, t * LANES : (t + 1) * LANES], lane, axis=1, mode="promise_in_bounds"
        )
        total = jnp.where(chunk == t, part, total)
    for c in range(3):
        tpos_sc[c * rows + at : c * rows + at + SLOTS, :] = jnp.broadcast_to(
            total[c : c + 1, :], (SLOTS, LANES)
        )


def geometry(idx, target, live, place_sc):
    lane = idx & (LANES - 1)
    chunk = idx >> 7
    chunks = place_sc.shape[1] // LANES
    offsets = []
    for c in range(3):
        total = jnp.zeros(idx.shape, f32)
        for t in range(chunks):
            table = jnp.broadcast_to(place_sc[c : c + 1, t * LANES : (t + 1) * LANES], idx.shape)
            part = jnp.take_along_axis(table, lane, axis=1, mode="promise_in_bounds")
            total = jnp.where(chunk == t, part, total)
        offsets.append(total - target[c])
    square = offsets[0] * offsets[0] + offsets[1] * offsets[1] + offsets[2] * offsets[2]
    distance = jnp.sqrt(jnp.where(live, square, 4.0))
    inverse = 1.0 / distance
    direction = [offset * inverse for offset in offsets]
    angle = (math.pi / CUTOFF) * distance
    sine = jnp.sin(angle)
    cosine = jnp.cos(angle)
    inside = live & (distance < CUTOFF)
    factor = jnp.where(inside, 0.5 * (cosine + 1.0), 0.0)
    slope = jnp.where(inside, (-0.5 * math.pi / CUTOFF) * sine, 0.0)
    return inverse, direction, sine, cosine, factor, slope


def fill_geometry(
    groups, blocks, owned, listed, hub_listed, hub_live, idx_sc, tpos_sc, place_sc, basis_sc, slope_sc, geo_sc, orders
):
    rows = idx_sc.shape[0]
    group = GROUP * SLOTS

    def step(i, carry):
        first = pl.multiple_of(i * group, SLOTS)

        def at(q):
            return pl.ds(pl.multiple_of(q * rows + first, SLOTS), group)

        row = iota((group, LANES), 0) + first
        block = row >> 4
        last = block == blocks
        valid = jnp.where(last, hub_live, owned - block * LANES)
        depth = jnp.where(last, hub_listed, listed)
        live = (iota((group, LANES), 1) < valid) & ((row & (SLOTS - 1)) < depth)
        inverse, direction, sine, cosine, factor, slope = geometry(
            idx_sc[pl.ds(first, group), :], [tpos_sc[at(c), :] for c in range(3)], live, place_sc
        )
        geo_sc[at(0), :] = factor
        for c in range(3):
            geo_sc[at(1 + c), :] = direction[c]
        geo_sc[at(4), :] = slope
        geo_sc[at(5), :] = inverse
        sine_n, cosine_n = sine, cosine
        for n in range(orders):
            ratio = sine_n * inverse
            basis_sc[at(n), :] = ratio.astype(bf16).astype(f32)
            if slope_sc is not None:
                slope_sc[at(n), :] = (((n + 1) * math.pi / CUTOFF) * cosine_n - ratio) * inverse
            if n + 1 < orders:
                sine_n, cosine_n = (
                    sine_n * cosine + cosine_n * sine,
                    cosine_n * cosine - sine_n * sine,
                )
        return carry

    lax.fori_loop(0, groups, step, 0)
    basis_sc[orders * rows : (orders + 2) * rows, :] = jnp.ones((2 * rows, LANES), f32)
    rest = (ORDER_ROWS - orders - 2) * rows
    basis_sc[(orders + 2) * rows :, :] = jnp.zeros((rest, LANES), f32)
    if slope_sc is not None:
        slope_sc[orders * rows :, :] = jnp.zeros((rest + 2 * rows, LANES), f32)


def unrolled(count, most):
    for size in range(most, 0, -1):
        if count % size == 0:
            return size
    return 1


def order_tiles(ref, row, rows):
    return [
        ref[pl.ds(row + t * TILE * rows, TILE, rows), :] for t in range(ORDER_ROWS // TILE)
    ]


def edge_coefficients(b, k, rows, basis_sc, geo_sc):
    row = b * SLOTS + k
    basis = order_tiles(basis_sc, row, rows)
    scale = [geo_sc[pl.ds(row + q * rows, 1), :] for q in range(4)]
    return basis, scale


def scaled_parts(basis, scale):
    plain = [part * scale[0] for part in basis]
    parts = []
    for c in range(3):
        parts += [part * scale[1 + c] for part in plain]
    return plain, parts


def make_filters(b, slots, rows, basis_sc, geo_sc, wext, filt, width):
    weights = wext[...]
    size = unrolled(slots, 5)
    for first in range(0, slots, size):
        turned = []
        for k in range(first, first + size):
            basis, scale = edge_coefficients(b, k, rows, basis_sc, geo_sc)
            plain, parts = scaled_parts(basis, scale)
            turned.append(jnp.concatenate(plain + parts, axis=0).T.astype(bf16))
        store_filters(first, turned, weights, filt, width)


def put_slot(filt, k, slot, value):
    filt[:, pl.ds(k * TILE * STEP + slot, TILE, STEP), :] = value.reshape(-1, TILE, LANES)


def get_slot(filt, k, slot):
    return filt[:, pl.ds(k * TILE * STEP + slot, TILE, STEP), :].reshape(LANES, LANES)


def store_filters(first, coeffs, weights, filt, width):
    product = mm(jnp.concatenate(coeffs, axis=0), weights)
    for n in range(len(coeffs)):
        for slot in range(7):
            column = 0 if slot < 3 else slot - 2
            put_slot(
                filt,
                first + n,
                slot,
                product[n * LANES : (n + 1) * LANES, column * width : (column + 1) * width],
            )


def fill_filters(slots, turned_sc, wext, filt, width, extra):
    weights = wext[...]
    size = unrolled(slots, 5)
    for first in range(0, slots, size):
        coeff = [turned_sc[k * LANES : (k + 1) * LANES, :] for k in range(first, first + size)]
        store_filters(first, coeff, weights, filt, width)
        for k in range(first, first + size):
            put_slot(filt, k, 7, extra(k))


def sigmoid(t):
    return 1.0 / (1.0 + jnp.exp(-t))


def message_net(rows, w1, b1, w2, b2):
    lead = rows[:, 0:LANES].astype(bf16)
    pre = mm(lead, w1) + b1
    gate = sigmoid(pre)
    hidden = (pre * gate).astype(bf16)
    filters = (mm(hidden, w2) + b2).astype(bf16).astype(f32)
    return lead, pre, gate, hidden, filters


def store_table(tiles, firsts, counts, rows, filters):
    gate = filters[:, 0:LANES]
    columns = [rows[:, (1 + c) * LANES : (2 + c) * LANES] * gate for c in range(3)]
    columns += [filters[:, LANES : 2 * LANES]] + [filters[:, 2 * LANES :]] * 3
    at = 0
    for first, count in zip(firsts, counts):
        for slot, column in enumerate(columns):
            tiles[pl.ds(first * TILE + slot, count, TILE), :] = column[at : at + count, :]
        at += count


def build_table(tiles, halo, arrived, w1, b1, w2, b2):
    counts = [up_to(h[1], TILE) for h in halo]
    firsts = [h[0] for h in halo]
    sides = jnp.concatenate([ref[0:count, :] for count, ref in zip(counts, arrived)], axis=0)
    store_table(tiles, firsts, counts, sides, message_net(sides, w1, b1, w2, b2)[4])


def tile_at(ref, row):
    return ref[pl.ds(pl.multiple_of(row * TILE, TILE), TILE), :]


def edge_at(k, n):
    return pl.ds((k * TILE + n) * STEP, TILE)


def source_at(ref, row):
    return ref[pl.ds(pl.multiple_of(row, TILE), TILE), :]


def sum_group(filt, tiles, flat, targets, sums, b, i, listed):
    first = b * LANES + i * TILE
    for n in range(TILE):
        total = None
        for k in range(listed):
            source = flat[first * SLOTS + k * TILE + n]
            part = source_at(tiles, source) * filt[i, edge_at(k, n), :]
            total = part if total is None else total + part
        sums[pl.ds(pl.multiple_of(targets[first + n], TILE), TILE), :] = total


def inner_kernel(
    listed,
    flat,
    targets,
    rows_ref,
    p_ref,
    table_ref,
    target_ref,
    w1_ref,
    b1_ref,
    w2_ref,
    b2_ref,
    wr_ref,
    br_ref,
    sums,
    tiles,
    filt,
    place_sc,
    idx_sc,
    tpos_sc,
    basis_sc,
    geo_sc,
    wext32,
    wext,
):
    owned = rows_ref.shape[0]
    orders = wr_ref.shape[0]
    rows = idx_sc.shape[0]
    place_sc[...] = jnp.zeros(place_sc.shape, f32)
    place_sc[:, 0:owned] = p_ref[...]
    build_radial(wext32, wext, wr_ref, br_ref)
    load_indices(idx_sc, tpos_sc, table_ref, target_ref)
    done = targets[TILE * LANES] // TILE
    each = LANES // TILE
    blocks = (done + each - 1) // each
    fill_geometry(
        (blocks + GROUP - 1) // GROUP,
        rows // SLOTS,
        owned,
        listed,
        0,
        0,
        idx_sc,
        tpos_sc,
        place_sc,
        basis_sc,
        None,
        geo_sc,
        orders,
    )
    own = rows_ref[...]
    weights = (w1_ref[...], b1_ref[...], w2_ref[...], b2_ref[...])
    store_table(tiles, [0], [owned], own, message_net(own, *weights)[4])
    sums[...] = jnp.zeros(sums.shape, f32)

    def regular_block(b, carry):
        make_filters(b, listed, rows, basis_sc, geo_sc, wext, filt, LANES)

        def atoms(i, inner):
            sum_group(filt, tiles, flat, targets, sums, b, i, listed)
            return inner

        lax.fori_loop(0, jnp.minimum(each, done - b * each), atoms, 0)
        return carry

    lax.fori_loop(0, blocks, regular_block, 0)


def forward_kernel(
    halo,
    shapes,
    listed,
    hub_listed,
    chunk,
    size_y,
    flat_table,
    flat_hub_table,
    targets,
    hub_list,
    hub_count,
    place_y,
    rows_ref,
    p_ref,
    cot_ref,
    table_ref,
    target_ref,
    hub_table_ref,
    hub_row_ref,
    sums_in,
    w1_ref,
    b1_ref,
    w2_ref,
    b2_ref,
    wr_ref,
    br_ref,
    u_ref,
    v_ref,
    w3_ref,
    b3_ref,
    w4_ref,
    b4_ref,
    *rest,
):
    arrived, rest = arrived_views([h[1] for h in halo[::2]], shapes, rest)
    (
        out_s_ref,
        out_v_ref,
        grad_ref,
        bias_ref,
        tiles,
        basis_sc,
        slope_sc,
        geo_sc,
    ) = rest[:8]
    share_refs = rest[8 : 8 + size_y]
    (
        filt,
        sums,
        place_sc,
        idx_sc,
        tpos_sc,
        wext32,
        wext,
        uv,
        out_sc,
        early_ref,
    ) = rest[8 + size_y :]
    owned = rows_ref.shape[0]
    width = LANES
    orders = wr_ref.shape[0]
    blocks = -(-owned // LANES)
    build_places(place_sc, p_ref, owned, halo, arrived)
    build_radial(wext32, wext, wr_ref, br_ref)
    load_indices(idx_sc, tpos_sc, table_ref, target_ref)
    load_hubs(idx_sc, tpos_sc, hub_table_ref, hub_row_ref, place_sc, owned)
    hub_live = hub_count[0]
    fill_geometry(
        -(-(blocks + 1) // GROUP), blocks, owned, listed, hub_listed, hub_live, idx_sc, tpos_sc, place_sc, basis_sc, slope_sc, geo_sc, orders
    )
    rows = idx_sc.shape[0]
    sums[...] = sums_in[...]
    weights = (w1_ref[...], b1_ref[...], w2_ref[...], b2_ref[...])
    own = rows_ref[...]
    store_table(tiles, [0], [owned], own, message_net(own, *weights)[4])
    build_table(tiles, halo, arrived, *weights)
    done = targets[TILE * LANES] // TILE
    each = LANES // TILE

    def regular_block(b, carry):
        make_filters(b, listed, rows, basis_sc, geo_sc, wext, filt, width)

        def atoms(i, inner):
            sum_group(filt, tiles, flat_table, targets, sums, b, i, listed)
            return inner

        start = jnp.maximum(done - b * each, 0)
        lax.fori_loop(start, jnp.minimum(each, owned // TILE - b * each), atoms, 0)
        return carry

    lax.fori_loop(done // each, blocks, regular_block, 0)
    hub_span = min(listed, up_to(hub_listed, 4))
    make_filters(blocks, hub_span, rows, basis_sc, geo_sc, wext, filt, width)

    def hub_slots(i, carry):
        for n in range(TILE):
            total = None
            for k in range(hub_listed):
                source = flat_hub_table[i * LANES + k * TILE + n]
                part = source_at(tiles, source) * filt[i, edge_at(k, n), :]
                total = part if total is None else total + part
            at = pl.ds(pl.multiple_of(hub_list[i * TILE + n] * TILE, TILE), TILE)
            sums[at, :] = sums[at, :] + total
        return carry

    lax.fori_loop(0, (hub_live + TILE - 1) // TILE, hub_slots, 0)

    uv[:, 0:width] = u_ref[...]
    uv[:, width:] = v_ref[...]
    early_ref[...] = jnp.zeros(early_ref.shape, f32)
    bias_ref[...] = jnp.zeros(bias_ref.shape, f32)

    def update(i, carry):
        first = pl.multiple_of(i * chunk, TILE)
        part = [sums[pl.ds(first * TILE + slot, chunk, TILE), :] for slot in range(7)]
        own = rows_ref[pl.ds(first, chunk), :]
        cot = cot_ref[pl.ds(first, chunk), :]
        state_s = own[:, 0:width] + part[3]
        state_v = [
            own[:, (1 + c) * width : (2 + c) * width] + (part[c] + part[4 + c]) for c in range(3)
        ]
        low = [x.astype(bf16) for x in state_v]
        both = [mm(x, uv[...]) for x in low]
        left = [x[:, 0:width] for x in both]
        right = [x[:, width:] for x in both]
        inner = left[0] * right[0] + left[1] * right[1] + left[2] * right[2]
        norm = jnp.sqrt(right[0] * right[0] + right[1] * right[1] + right[2] * right[2] + 1.0)
        joined = jnp.concatenate([state_s, norm], axis=1).astype(bf16)
        pre = mm(joined, w3_ref[...]) + b3_ref[...]
        gate = sigmoid(pre)
        hidden = (pre * gate).astype(bf16)
        amp = mm(hidden, w4_ref[...]) + b4_ref[...]
        amp_vv = amp[:, 0:width]
        amp_sv = amp[:, width : 2 * width]
        amp_ss = amp[:, 2 * width :]
        out_sc[pl.ds(first, chunk), 0:width] = state_s + amp_sv * inner + amp_ss
        for c in range(3):
            out_sc[pl.ds(first, chunk), (1 + c) * width : (2 + c) * width] = (
                state_v[c] + amp_vv * left[c]
            )
        gs = cot[:, 0:width]
        gv = [cot[:, (1 + c) * width : (2 + c) * width] for c in range(3)]
        grad_amp = jnp.concatenate(
            [gv[0] * left[0] + gv[1] * left[1] + gv[2] * left[2], gs * inner, gs], axis=1
        )
        grad_amp_low = grad_amp.astype(bf16)
        grad_w4 = mm(hidden, grad_amp_low, TN)
        for t in range(3):
            early_ref[(4 + t) * width : (5 + t) * width, :] += grad_w4[:, t * width : (t + 1) * width]
            bias_ref[1 + t : 2 + t, :] += jnp.sum(
                grad_amp[:, t * width : (t + 1) * width], axis=0, keepdims=True
            )
        slope = gate * (1.0 + pre * (1.0 - gate))
        grad_pre = mm(grad_amp_low, w4_ref[...], NT) * slope
        bias_ref[0:1, :] += jnp.sum(grad_pre, axis=0, keepdims=True)
        grad_pre_low = grad_pre.astype(bf16)
        early_ref[2 * width : 4 * width, :] += mm(joined, grad_pre_low, TN)
        grad_joined = mm(grad_pre_low, w3_ref[...], NT)
        mixed = gs * amp_sv
        ratio = grad_joined[:, width:] / norm
        grad_ref[pl.ds(first * TILE + 3, chunk, TILE), :] = gs + grad_joined[:, 0:width]
        grad_ref[pl.ds(first * TILE + 7, chunk, TILE), :] = jnp.ones((chunk, width), f32)
        grad_uv = None
        for c in range(3):
            grad_left = gv[c] * amp_vv + mixed * right[c]
            grad_right = mixed * left[c] + ratio * right[c]
            grad_both = jnp.concatenate([grad_left, grad_right], axis=1).astype(bf16)
            piece = mm(low[c], grad_both, TN)
            grad_uv = piece if grad_uv is None else grad_uv + piece
            grad_v = gv[c] + mm(grad_both, uv[...], NT)
            grad_ref[pl.ds(first * TILE + c, chunk, TILE), :] = grad_v
            grad_ref[pl.ds(first * TILE + 4 + c, chunk, TILE), :] = grad_v
        early_ref[0:width, :] += grad_uv[:, 0:width]
        early_ref[width : 2 * width, :] += grad_uv[:, width:]
        return carry

    lax.fori_loop(0, owned // chunk, update, 0)
    out_s_ref[...] = out_sc[:, 0:width].astype(bf16)
    out_v_ref[...] = out_sc[:, width:].astype(bf16)
    give_shares(place_y[0], early_ref, share_refs)


def places_of(sums, first, count):
    select = (iota((TILE, LANES), 0) == (iota((TILE, LANES), 1) & 7)).astype(bf16)
    value = sums[pl.ds(first * TILE + 7, count, TILE), :]
    high, middle, low = thirds(value)
    return (mm(select, high, NT) + mm(select, middle, NT)) + mm(select, low, NT)


def message_back(late_ref, weights, rows, part, own_grads):
    w1, b1, w2, b2 = weights
    width = LANES
    bias_at = 4 * width + 3 * ORDER_ROWS
    lead, pre, gate, hidden, filters = message_net(rows, w1, b1, w2, b2)
    vec = [rows[:, (1 + c) * width : (2 + c) * width] for c in range(3)]
    grad_filters = jnp.concatenate(
        [
            vec[0] * part[0] + vec[1] * part[1] + vec[2] * part[2],
            part[3],
            part[4] + part[5] + part[6],
        ],
        axis=1,
    )
    low = grad_filters.astype(bf16)
    grad_w2 = mm(hidden, low, TN)
    for t in range(3):
        late_ref[(1 + t) * width : (2 + t) * width, :] += grad_w2[:, t * width : (t + 1) * width]
        at = bias_at + 1 + t
        late_ref[at : at + 1, :] += jnp.sum(
            grad_filters[:, t * width : (t + 1) * width], axis=0, keepdims=True
        )
    grad_pre = mm(low, w2, NT) * (gate * (1.0 + pre * (1.0 - gate)))
    late_ref[bias_at : bias_at + 1, :] += jnp.sum(grad_pre, axis=0, keepdims=True)
    grad_pre_low = grad_pre.astype(bf16)
    late_ref[0:width, :] += mm(lead, grad_pre_low, TN)
    gate_vv = filters[:, 0:width]
    grads = [mm(grad_pre_low, w1, NT)] + [gate_vv * part[c] for c in range(3)]
    if own_grads is None:
        return grads
    return [x + y for x, y in zip(grads, own_grads)]


def backward_kernel(
    halo,
    shapes,
    listed,
    hub_listed,
    flat_table,
    flat_hub_table,
    targets,
    hub_list,
    hub_count,
    grads,
    bias_ref,
    tiles,
    basis_sc,
    slope_sc,
    geo_sc,
    w1_ref,
    b1_ref,
    w2_ref,
    b2_ref,
    wr_ref,
    br_ref,
    *rest,
):
    arrived, rest = arrived_views([h[1] for h in halo[::2]], shapes, rest)
    sums, target_sc, late_ref = rest[:3]
    rest = rest[3:]
    packets = rest[4 : 4 + shapes[2]]
    side_refs = list(rest[:4]) + pair_views(packets, packed_rows(halo[4][1]))
    rest = rest[4 + shapes[2] :]
    (
        filt,
        wext32,
        wext,
        turned_sc,
        coeff_sc,
        mix_sc,
        reduce_sc,
        spread_sc,
        radial_sc,
    ) = rest
    owned = grads.shape[0] // TILE
    width = LANES
    orders = wr_ref.shape[0]
    blocks = -(-owned // LANES)
    build_radial(wext32, wext, wr_ref, br_ref)
    hub_live = hub_count[0]
    rows = geo_sc.shape[0] // 6
    weights = (w1_ref[...], b1_ref[...], w2_ref[...], b2_ref[...])
    sums[...] = jnp.zeros(sums.shape, f32)
    radial_sc[...] = jnp.zeros(radial_sc.shape, f32)
    spread_sc[...] = jnp.zeros(spread_sc.shape, f32)
    reduce_sc[...] = jnp.zeros(reduce_sc.shape, f32)
    late_ref[...] = jnp.zeros(late_ref.shape, f32)

    def block_grads(b, count, trips, source_of, target_of):
        def mixes(pair, inner):
            for part in range(PARTS):
                i = pair * PARTS + part
                for n in range(TILE):
                    grad = source_at(grads, target_of(i, n))
                    for k in range(count):
                        filt[i, edge_at(k, n), :] = grad * source_at(tiles, source_of(i, k, n))
            return inner

        lax.fori_loop(0, trips, mixes, 0)
        span = min(listed, up_to(count, 4)) if count != listed else listed
        size = unrolled(span, 5)
        step = size * LANES

        def analyse(i, carry):
            first = i * step
            loaded = []
            for n in range(size):
                k = i * size + n
                part = [get_slot(filt, k, slot) for slot in range(7)]
                at = pl.ds(k * LANES, LANES)
                mix = [part[0] + part[1] + part[2], part[3], part[4], part[5], part[6]]
                for q in range(5):
                    mix_sc[at, q * width : (q + 1) * width] = mix[q].astype(bf16)
                row = b * SLOTS + k
                basis, scale = edge_coefficients(b, k, rows, basis_sc, geo_sc)
                loaded.append((basis, scale, order_tiles(slope_sc, row, rows)))
                plain, parts = scaled_parts(basis, scale)
                coeff = jnp.concatenate(plain + parts, axis=0)
                coeff_sc[:, at] = coeff.astype(bf16)
                turned_sc[at, :] = coeff.T.astype(bf16)
            mixes = mix_sc[pl.ds(first, step), :]
            backs = mm(wext[...], mixes, NT)
            radial_sc[...] += mm(coeff_sc[:, pl.ds(first, step)], mixes)
            for n, (basis, scale, slopes) in enumerate(loaded):
                back = backs[:, n * LANES : (n + 1) * LANES]
                total = None
                for t in range(ORDER_ROWS // TILE):
                    pieces = [
                        back[j * ORDER_ROWS + t * TILE : j * ORDER_ROWS + (t + 1) * TILE, :]
                        for j in range(4)
                    ]
                    mixed = (
                        pieces[0]
                        + pieces[1] * scale[1]
                        + pieces[2] * scale[2]
                        + pieces[3] * scale[3]
                    )
                    values = [mixed * basis[t], mixed * slopes[t]] + [
                        pieces[1 + c] * basis[t] for c in range(3)
                    ]
                    total = values if total is None else [x + y for x, y in zip(total, values)]
                for q in range(5):
                    at = q * TILE * SLOTS + i * size + n
                    reduce_sc[pl.ds(at, TILE, SLOTS), :] = total[q]
            return carry

        for i in range(span // size):
            analyse(i, 0)

        def geo(q):
            return geo_sc[pl.ds(pl.multiple_of(q * rows + b * SLOTS, SLOTS), SLOTS), :]

        factor = geo(0)
        direction = [geo(1 + c) for c in range(3)]
        slope = geo(4)
        inverse = geo(5)
        red = []
        for q in range(5):
            at = q * TILE * SLOTS
            pieces = [reduce_sc[at + n * SLOTS : at + (n + 1) * SLOTS] for n in range(TILE)]
            red.append(sum(pieces[1:], pieces[0]))
        grad_d = factor * red[1] + slope * red[0]
        grad_u = [factor * red[2 + c] for c in range(3)]
        along = (
            direction[0] * grad_u[0] + direction[1] * grad_u[1] + direction[2] * grad_u[2]
        )
        row = iota((SLOTS, LANES), 0)
        for c in range(3):
            value = (grad_u[c] - direction[c] * along) * inverse + grad_d * direction[c]
            value = jnp.where(row < count, value, 0.0)
            spread_sc[pl.ds(c, SLOTS, TILE), :] = value
            target_sc[b, c : c + 1, :] = -jnp.sum(value, axis=0, keepdims=True)
        turned = spread_sc[...].T
        group_of = iota((LANES, LANES), 1) >> 3
        fill_filters(
            span, turned_sc, wext, filt, width, lambda k: jnp.where(group_of == k, turned, 0.0)
        )

        def scatter(pair, inner):
            for part in range(PARTS):
                i = pair * PARTS + part
                for n in range(TILE):
                    grad = source_at(grads, target_of(i, n))
                    places = [
                        pl.ds(pl.multiple_of(source_of(i, k, n), TILE), TILE)
                        for k in range(count)
                    ]
                    held = [sums[at, :] for at in places]
                    fresh = [held[k] + grad * filt[i, edge_at(k, n), :] for k in range(count)]
                    for k in range(count):
                        sums[places[k], :] = fresh[k]
            return inner

        lax.fori_loop(0, trips, scatter, 0)

    target_sc[...] = jnp.zeros(target_sc.shape, f32)

    def regular_block(b, carry):
        base = b * LANES
        block_grads(
            b,
            listed,
            (jnp.minimum(LANES, owned - base) + PARTS * TILE - 1) // (PARTS * TILE),
            lambda i, k, n: flat_table[(base + i * TILE) * SLOTS + k * TILE + n],
            lambda i, n: targets[base + i * TILE + n],
        )
        return carry

    lax.fori_loop(0, blocks, regular_block, 0)
    block_grads(
        blocks,
        hub_listed,
        (hub_live + PARTS * TILE - 1) // (PARTS * TILE),
        lambda i, k, n: flat_hub_table[i * LANES + k * TILE + n],
        lambda i, n: hub_list[i * TILE + n] * TILE,
    )

    bias_at = 4 * width + 3 * ORDER_ROWS
    side_parts = []
    for first, count, _, _ in halo:
        count8 = up_to(count, TILE)
        part = [sums[pl.ds(first * TILE + slot, count8, TILE), :] for slot in range(7)]
        if count8 != count:
            keep = iota((count8, 1), 0) < count
            part = [jnp.where(keep, x, 0.0) for x in part]
        side_parts.append(part)
    side_rows = jnp.concatenate(
        [ref[0 : up_to(h[1], TILE), :] for h, ref in zip(halo, arrived)], axis=0
    )
    side_grads = message_back(
        late_ref, weights, side_rows, [jnp.concatenate(x, axis=0) for x in zip(*side_parts)], None
    )
    at = 0
    for index, (first, count, _, _) in enumerate(halo):
        count8 = up_to(count, TILE)
        side_ref = side_refs[index]
        side_ref[...] = jnp.zeros(side_ref.shape, f32)
        for q in range(4):
            side_ref[0:count8, q * width : (q + 1) * width] = side_grads[q][at : at + count8, :]
        at += count8
        write_places(side_ref, count, places_of(sums, first, count))

    for t in range(3):
        if t < 2:
            value = radial_sc[0:orders, t * width : (t + 1) * width]
            bias = radial_sc[orders : orders + 1, t * width : (t + 1) * width]
        else:
            value = None
            bias = None
            for c in range(3):
                at = (1 + c) * ORDER_ROWS
                lanes = slice((2 + c) * width, (3 + c) * width)
                one = radial_sc[at : at + orders, lanes]
                two = radial_sc[at + orders : at + orders + 1, lanes]
                value = one if value is None else value + one
                bias = two if bias is None else bias + two
        late_ref[4 * width + t * ORDER_ROWS : 4 * width + t * ORDER_ROWS + orders, :] = value
        late_ref[bias_at + 4 + t : bias_at + 5 + t, :] = bias

    late_ref[bias_at + 7 : bias_at + 11, :] = bias_ref[0:4, :]


def own_back_kernel(
    shares,
    me,
    sums,
    target_ref,
    late_in,
    s_ref,
    v_ref,
    grads,
    names_ref,
    hub_row_ref,
    w1_ref,
    b1_ref,
    w2_ref,
    b2_ref,
    *rest,
):
    early, rest = rest[:shares], rest[shares:]
    own_ref, place_ref, early_ref = rest[:3]
    share_refs, late_ref = rest[3:-1], rest[-1]
    early_ref[...] = summed(early)
    owned = s_ref.shape[0]
    rows = jnp.concatenate([s_ref[...].astype(f32), v_ref[...].astype(f32)], axis=1)
    width = LANES
    hubs = hub_row_ref.shape[1]
    blocks = -(-owned // LANES)
    weights = (w1_ref[...], b1_ref[...], w2_ref[...], b2_ref[...])
    late_ref[...] = late_in[...]
    parts = [sums[pl.ds(slot, owned, TILE), :] for slot in range(7)]
    held = [grads[pl.ds(slot, owned, TILE), :] for slot in (3, 0, 1, 2)]
    own_grads = message_back(late_ref, weights, rows, parts, held)
    for q in range(4):
        own_ref[:, q * width : (q + 1) * width] = own_grads[q]
    give_shares(me[0], late_ref, share_refs)
    place_ref[...] = places_of(sums, 0, owned)
    total = None
    for b in range(blocks + 1):
        names = hub_row_ref[...] * TILE if b == blocks else names_ref[b : b + 1, :]
        onehot = (iota((owned, hubs), 0) * TILE == jnp.broadcast_to(names, (owned, hubs))).astype(bf16)
        part = pick_exact(target_ref[b], onehot)
        total = part if total is None else total + part
    place_ref[...] += total


def chunk_of(ref, me, shift, count):
    size = ref.shape[0] // count
    at = lax.rem(me + shift, count) * size
    return ref[pl.ds(pl.multiple_of(at, TILE), size), :]


def give_shares(me, ref, share_refs):
    for t, share_ref in enumerate(share_refs):
        share_ref[...] = chunk_of(ref, me, t, len(share_refs))


def gathered_back(first, count, pieces):
    rows = sum(list_ref.shape[1] for _, list_ref, _ in pieces)
    target = iota((count, rows), 0) + first
    names = jnp.concatenate(
        [
            jnp.broadcast_to(list_ref[side : side + 1, :], (TILE, list_ref.shape[1]))
            for _, list_ref, side in pieces
        ],
        axis=1,
    )
    onehot = (target == names[0:1, :]).astype(bf16)
    values = jnp.concatenate(
        [ref[0 : list_ref.shape[1], :] for ref, list_ref, _ in pieces], axis=0
    ).astype(bf16)
    places = jnp.concatenate(
        [read_places(ref, list_ref.shape[1])[:, 0 : list_ref.shape[1]] for ref, list_ref, _ in pieces],
        axis=1,
    )
    return mm(onehot, values), pick_exact(places, onehot)


def list_pieces(lists, arrived):
    pieces = []
    for n, list_ref in enumerate(lists):
        pieces += [(arrived[2 * n], list_ref, 0), (arrived[2 * n + 1], list_ref, 1)]
    return pieces


def add_back(first, count, pieces, part_ref, out_ref):
    count8 = up_to(count, TILE)
    total, places = gathered_back(first, count8, pieces)
    if count8 != count:
        total = jnp.where(iota((count8, 1), 0) < count, total, 0.0)
    rows = part_ref.shape[0]
    out_ref[0:rows, :] = part_ref[...]
    out_ref[0:count8, :] += total
    write_places(out_ref, count, read_places(part_ref, count)[:, 0:count] + places[:, 0:count])


def return_y_kernel(ranges, sizes, me, z_list, *refs):
    size_z, size_y = sizes
    z_size = 1 if size_z == 2 else 2
    y_size = 1 if size_y == 2 else 2
    packets, refs = refs[:z_size], refs[z_size:]
    late, refs = refs[:size_y], refs[size_y:]
    early, refs = refs[0], refs[1:]
    partial, refs = refs[:2], refs[2:]
    outs, refs = refs[:y_size], refs[y_size:]
    share_refs, share = refs[:-1], refs[-1]
    size = late[0].shape[0]
    share[0:size, :] = summed(late)
    share[size:, :] = early[...]
    give_shares(me[0], share, share_refs)
    arrived, _ = arrived_views([z_list.shape[1]], [z_size], packets)
    pieces = list_pieces([z_list], arrived)
    y_rows = packed_rows(ranges[0][1])
    for (first, count), part_ref, out_ref in zip(ranges, partial, pair_views(outs, y_rows)):
        add_back(first, count, pieces, part_ref, out_ref)


def return_x_kernel(ranges, sizes, z_list, y_list, *refs):
    size_z, size_y = sizes
    shapes = [1 if size == 2 else 2 for size in sizes]
    arrived, rest = arrived_views([z_list.shape[1], y_list.shape[1]], shapes, refs)
    shares, rest = rest[:size_z], rest[size_z:]
    partial, rest = rest[:2], rest[2:]
    outs, keep_x = rest[:-1], rest[-1]
    keep_x[...] = summed(shares)
    x_rows = packed_rows(ranges[0][1])
    pieces = list_pieces([z_list, y_list], arrived)
    for (first, count), part_ref, out_ref in zip(ranges, partial, pair_views(outs, x_rows)):
        add_back(first, count, pieces, part_ref, out_ref)


def own_kernel(shapes, *refs):
    phases = len(shapes)
    lists = refs[:phases]
    arrived, rest = arrived_views([x.shape[1] for x in lists], shapes, refs[phases:])
    own_ref, place_ref, *outs = rest
    total, places = gathered_back(0, own_ref.shape[0], list_pieces(lists, arrived))
    total = total + own_ref[...]
    places = places + place_ref[...]
    if len(outs) == 2:
        outs[0][...] = total
        outs[1][...] = places
    else:
        outs[0][...] = total[:, 0:LANES]
        outs[1][...] = total[:, LANES:]
        outs[2][...] = places[0:3, :]


def summed(refs):
    total = refs[0][...]
    for ref in refs[1:]:
        total = total + ref[...]
    return total


def sum_kernel(*refs):
    refs[-1][...] = summed(refs[:-1])


def join_kernel(me, *refs):
    shares, out_ref = refs[:-1], refs[-1]
    count = len(shares)
    size = shares[0].shape[0]
    for t in range(count):
        at = lax.rem(me[0] + count - t, count) * size
        out_ref[pl.ds(pl.multiple_of(at, TILE), size), :] = shares[t][...]


def gather_order(me, count):
    if count != 4:
        return [lax.rem(me + count - t, count) for t in range(count)]
    beside = me + 1 - 2 * lax.rem(me, 2)
    return [me, beside, lax.rem(me + 2, 4), lax.rem(beside + 2, 4)]


def unpack_kernel(sizes, late_share, me, *refs):
    size_y, size_z = sizes
    late_ref, early_ref, joined = refs[-3:]
    outs = refs[size_y:-3]
    share = late_share + early_ref.shape[0] // size_y
    for t, owner in enumerate(gather_order(me[0], size_y)):
        joined[pl.ds(pl.multiple_of(owner * share, TILE), share), :] = refs[t][...]
    rest = share - late_share
    for n in range(size_y):
        late_ref[n * late_share : (n + 1) * late_share, :] = joined[
            n * share : n * share + late_share, :
        ]
        early_ref[n * rest : (n + 1) * rest, :] = joined[n * share + late_share : (n + 1) * share, :]
    (w1, b1, w2, b2, wr, br, u, v, w3, b3, w4, b4) = outs
    width = LANES
    orders = wr.shape[0]
    bias_at = 4 * width + 3 * ORDER_ROWS
    u[...] = early_ref[0:width, :]
    v[...] = early_ref[width : 2 * width, :]
    w3[...] = early_ref[2 * width : 4 * width, :]
    b3[...] = late_ref[bias_at + 7, :]
    w1[...] = late_ref[0:width, :]
    b1[...] = late_ref[bias_at, :]
    for t in range(3):
        lanes = slice(t * width, (t + 1) * width)
        w4[:, lanes] = early_ref[(4 + t) * width : (5 + t) * width, :]
        b4[lanes] = late_ref[bias_at + 8 + t, :]
        w2[:, lanes] = late_ref[(1 + t) * width : (2 + t) * width, :]
        b2[lanes] = late_ref[bias_at + 1 + t, :]
        at = 4 * width + t * ORDER_ROWS
        wr[:, lanes] = late_ref[at : at + orders, :]
        br[lanes] = late_ref[bias_at + 4 + t, :]


def work(array, operations):
    return pl.CostEstimate(
        flops=operations, bytes_accessed=4 * array.size * array.dtype.itemsize, transcendentals=0
    )


def exchange(axis, packets):
    count = lax.axis_size(axis)
    up = [(i, (i + 1) % count) for i in range(count)]
    if len(packets) == 1:
        return [lax.ppermute(packets[0], axis, up)]
    down = [(j, i) for i, j in up]
    return [lax.ppermute(packets[1], axis, up), lax.ppermute(packets[0], axis, down)]


def rotated(axis, pieces):
    count = lax.axis_size(axis)
    return [pieces[0]] + [
        lax.ppermute(pieces[t], axis, [(i, (i + t) % count) for i in range(count)])
        for t in range(1, count)
    ]


def gathered(axis, piece):
    if lax.axis_size(axis) != 4:
        return rotated(axis, [piece] * lax.axis_size(axis))
    beside = [(i, i ^ 1) for i in range(4)]
    across = lax.ppermute(piece, axis, [(i, (i + 2) % 4) for i in range(4)])
    near = lax.ppermute(piece, axis, beside)
    return [piece, near, across, lax.ppermute(across, axis, beside)]


def local(
    scalar_feat,
    vector_feat,
    positions,
    message_inner,
    message_inner_bias,
    message_outer,
    message_outer_bias,
    radial_weight,
    radial_bias,
    update_left,
    update_right,
    update_inner,
    update_inner_bias,
    update_outer,
    update_outer_bias,
    scalar_cotangent,
    vector_cotangent,
    x_face_rows,
    y_face_rows,
    z_face_rows,
    neighbour_table,
    hub_atoms,
    hub_table,
    hub_count,
):
    owned, width = scalar_feat.shape
    length = G * SPACING
    counts = [x_face_rows.shape[2], y_face_rows.shape[2], z_face_rows.shape[2]]
    lists = [x_face_rows[0], y_face_rows[0], z_face_rows[0]]
    axes = ("gx", "gy", "gz")
    halo = []
    first = owned
    for number, count in enumerate(counts):
        halo.append((first, count, number, -length))
        halo.append((first + count, count, number, length))
        first += 2 * count
    ext = first
    packets, (rows, place, y_list, z_list) = first_pack(
        axes[0], lists, scalar_feat, vector_feat, positions
    )
    lists = [lists[0], y_list, z_list]
    arrived = exchange(axes[0], packets)
    shapes = [len(packets)]
    own_packs = pack_own(lists[1:], rows, place)
    table, flat_table, flat_hub_table, names, target_place = order_atoms(
        neighbour_table, hub_table, place
    )
    for number in range(1, 3):
        own = own_packs[2 * number - 2 : 2 * number]
        packets = pack_sides(
            axes[number], lists[number], own, halo[: 2 * number], shapes, arrived
        )
        packets, names = lax.optimization_barrier((packets, names))
        arrived = arrived + exchange(axes[number], packets)
        shapes.append(len(packets))
    shapes = tuple(shapes)

    cots = jnp.concatenate([scalar_cotangent, vector_cotangent], axis=1).astype(f32)
    flat_table = flat_table.reshape(-1)
    flat_hub_table = flat_hub_table.reshape(-1)
    targets = names.reshape(-1)
    hub_row = hub_atoms.reshape(1, -1)
    b1 = message_inner_bias.reshape(1, -1)
    b2 = message_outer_bias.reshape(1, -1)
    br = radial_bias.reshape(1, -1)
    b3 = update_inner_bias.reshape(1, -1)
    b4 = update_outer_bias.reshape(1, -1)

    blocks = -(-owned // LANES)
    chunk = owned
    ext_tiles = up_to(ext, TILE) * TILE
    slots = neighbour_table.shape[0]
    assert slots <= SLOTS and hub_table.shape[0] <= slots and owned % TILE == 0
    assert hub_atoms.shape[0] == LANES and blocks <= TILE
    hub_slots = hub_table.shape[0]
    inner_rows = up_to(blocks, GROUP) * SLOTS
    smem = pl.BlockSpec(memory_space=pltpu.SMEM)
    vmem = pl.BlockSpec(memory_space=pltpu.VMEM)
    small = pltpu.CompilerParams(vmem_limit_bytes=8 * MIB)
    middle = pltpu.CompilerParams(vmem_limit_bytes=20 * MIB)
    wide = 5 * width
    size_x, size_y, size_z = [lax.axis_size(axis) for axis in axes]
    step = TILE * size_y * size_z
    late_rows = up_to(4 * width + 3 * ORDER_ROWS + 2 * TILE, step)
    early_rows = up_to(7 * width, step)
    late_share = jax.ShapeDtypeStruct((late_rows // size_y, width), f32)
    early_share = jax.ShapeDtypeStruct((early_rows // size_y, width), f32)
    share_y = jax.ShapeDtypeStruct(((late_rows + early_rows) // size_y, width), f32)
    share_z = jax.ShapeDtypeStruct((share_y.shape[0] // size_z, width), f32)
    me_y = lax.axis_index("gy").reshape(1)
    me_z = lax.axis_index("gz").reshape(1)
    geo_rows = up_to(blocks + 1, GROUP) * SLOTS
    shared = [
        pltpu.VMEM((TILE, up_to(ext, LANES)), f32),
        pltpu.VMEM((geo_rows, LANES), jnp.int32),
        pltpu.VMEM((3 * geo_rows, LANES), f32),
    ]
    inner_sums = pl.pallas_call(
        functools.partial(inner_kernel, slots),
        in_specs=[smem] * 2 + [vmem] * 10,
        out_shape=jax.ShapeDtypeStruct((owned * TILE, LANES), f32),
        scratch_shapes=[
            pltpu.VMEM((owned * TILE, LANES), f32),
            pltpu.VMEM((LANES // TILE, slots * TILE * STEP, LANES), f32),
            pltpu.VMEM((TILE, blocks * LANES), f32),
            pltpu.VMEM((inner_rows, LANES), jnp.int32),
            pltpu.VMEM((3 * inner_rows, LANES), f32),
            pltpu.VMEM((ORDER_ROWS * inner_rows, LANES), f32),
            pltpu.VMEM((6 * inner_rows, LANES), f32),
            pltpu.VMEM((4 * ORDER_ROWS, wide), f32),
            pltpu.VMEM((4 * ORDER_ROWS, wide), bf16),
        ],
        compiler_params=pltpu.CompilerParams(vmem_limit_bytes=24 * MIB),
        cost_estimate=work(rows, 2 * geo_rows * LANES * 4 * ORDER_ROWS * wide * 3),
        name="edges_inner",
    )(
        flat_table,
        targets,
        rows,
        place,
        table,
        target_place,
        message_inner,
        b1,
        message_outer,
        b2,
        radial_weight,
        br,
    )
    out_s, out_v, grad, bias, *tables = pl.pallas_call(
        functools.partial(
            forward_kernel, tuple(halo), shapes, slots, hub_slots, chunk, size_y
        ),
        in_specs=[smem] * 6 + [vmem] * (20 + len(arrived)),
        out_shape=(
            jax.ShapeDtypeStruct((owned, width), bf16),
            jax.ShapeDtypeStruct((owned, 3 * width), bf16),
            jax.ShapeDtypeStruct((owned * TILE, width), f32),
            jax.ShapeDtypeStruct((TILE, width), f32),
            jax.ShapeDtypeStruct((ext_tiles, LANES), f32),
            jax.ShapeDtypeStruct((ORDER_ROWS * geo_rows, LANES), f32),
            jax.ShapeDtypeStruct((ORDER_ROWS * geo_rows, LANES), f32),
            jax.ShapeDtypeStruct((6 * geo_rows, LANES), f32),
        )
        + (early_share,) * size_y,
        scratch_shapes=[
            pltpu.VMEM((LANES // TILE, slots * TILE * STEP, LANES), f32),
            pltpu.VMEM((owned * TILE, LANES), f32),
        ]
        + shared
        + [
            pltpu.VMEM((4 * ORDER_ROWS, wide), f32),
            pltpu.VMEM((4 * ORDER_ROWS, wide), bf16),
            pltpu.VMEM((width, 2 * width), bf16),
            pltpu.VMEM((owned, 4 * width), f32),
            pltpu.VMEM((early_rows, width), f32),
        ],
        compiler_params=pltpu.CompilerParams(vmem_limit_bytes=24 * MIB),
        name="edges_forward",
    )(
        flat_table,
        flat_hub_table,
        targets,
        hub_atoms,
        hub_count,
        me_y,
        rows,
        place,
        cots,
        table,
        target_place,
        hub_table,
        hub_row,
        inner_sums,
        message_inner,
        b1,
        message_outer,
        b2,
        radial_weight,
        br,
        update_left,
        update_right,
        update_inner,
        b3,
        update_outer,
        b4,
        *arrived,
    )
    tables, early = tables[:4], rotated("gy", tables[4:])
    results = pl.pallas_call(
        functools.partial(backward_kernel, tuple(halo), shapes, slots, hub_slots),
        in_specs=[smem] * 5 + [vmem] * (12 + len(arrived)),
        out_shape=(
            jax.ShapeDtypeStruct((ext_tiles, LANES), f32),
            jax.ShapeDtypeStruct((blocks + 1, TILE, LANES), f32),
            jax.ShapeDtypeStruct((late_rows, width), f32),
        )
        + tuple(
            jax.ShapeDtypeStruct((packed_rows(count), 4 * width), f32)
            for count in (counts[0], counts[0], counts[1], counts[1])
        )
        + tuple(packet_shapes("gz", counts[2], 4 * width, 0)),
        scratch_shapes=[
            pltpu.VMEM((LANES // TILE, slots * TILE * STEP, LANES), f32),
            pltpu.VMEM((4 * ORDER_ROWS, wide), f32),
            pltpu.VMEM((4 * ORDER_ROWS, wide), bf16),
            pltpu.VMEM((slots * LANES, 4 * ORDER_ROWS), bf16),
            pltpu.VMEM((4 * ORDER_ROWS, slots * LANES), bf16),
            pltpu.VMEM((slots * LANES, wide), bf16),
            pltpu.VMEM((5 * TILE * SLOTS, LANES), f32),
            pltpu.VMEM((LANES, LANES), f32),
            pltpu.VMEM((4 * ORDER_ROWS, wide), f32),
        ],
        compiler_params=pltpu.CompilerParams(vmem_limit_bytes=22 * MIB),
        cost_estimate=work(rows, 2 * geo_rows * LANES * 4 * ORDER_ROWS * wide * 12),
        name="edges_backward",
    )(
        flat_table,
        flat_hub_table,
        targets,
        hub_atoms,
        hub_count,
        grad,
        bias,
        *tables,
        message_inner,
        b1,
        message_outer,
        b2,
        radial_weight,
        br,
        *arrived,
    )
    sums, target, late = results[:3]
    sides = results[3:7]
    packets, early = lax.optimization_barrier((results[7:], early))
    back_z = exchange("gz", packets)
    own, place, early, *late = pl.pallas_call(
        functools.partial(own_back_kernel, size_y),
        in_specs=[smem] + [vmem] * (12 + size_y),
        out_shape=(
            jax.ShapeDtypeStruct((owned, 4 * width), f32),
            jax.ShapeDtypeStruct((TILE, owned), f32),
            early_share,
        )
        + (late_share,) * size_y,
        scratch_shapes=[pltpu.VMEM((late_rows, width), f32)],
        compiler_params=pltpu.CompilerParams(vmem_limit_bytes=14 * MIB),
        name="own_backward",
    )(me_y, sums, target, late, scalar_feat, vector_feat, grad, names, hub_row, message_inner, b1, message_outer, b2, *early)
    ranges = [(h[0], h[1]) for h in halo]

    late = rotated("gy", late)
    results = pl.pallas_call(
        functools.partial(return_y_kernel, tuple(ranges[2:4]), (size_z, size_y)),
        in_specs=[smem] + [vmem] * (1 + shapes[2] + size_y + 3),
        out_shape=tuple(packet_shapes("gy", counts[1], 4 * width, 0)) + (share_z,) * size_z,
        scratch_shapes=[pltpu.VMEM(share_y.shape, f32)],
        compiler_params=middle,
        name="return_y",
    )(me_z, lists[2], *back_z, *late, early, *sides[2:4])
    packets, shares = results[: shapes[1]], results[shapes[1] :]

    shares = rotated("gz", shares)
    back_y = exchange("gy", packets)
    results = pl.pallas_call(
        functools.partial(return_x_kernel, tuple(ranges[0:2]), (size_z, size_y)),
        out_shape=tuple(packet_shapes("gx", counts[0], 4 * width, 0)) + (share_z,),
        compiler_params=middle,
        name="return_x",
    )(lists[2], lists[1], *back_z, *back_y, *shares, *sides[0:2])
    packets, keep = results[:-1], results[-1]

    shares = rotated("gx", [keep] * size_x)
    total = pl.pallas_call(
        sum_kernel, out_shape=share_z, compiler_params=small, name="sum_last"
    )(*shares)
    packets, total = lax.optimization_barrier((packets, total))
    shares = rotated("gz", [total] * size_z)
    back_x = exchange("gx", packets)
    own, place = pl.pallas_call(
        functools.partial(own_kernel, (shapes[2], shapes[1])),
        out_shape=(
            jax.ShapeDtypeStruct(own.shape, f32),
            jax.ShapeDtypeStruct(place.shape, f32),
        ),
        compiler_params=middle,
        cost_estimate=work(own, 2 * owned * 4 * width * 1056),
        name="own_partial",
    )(lists[2], lists[1], *back_z, *back_y, own, place)
    total = pl.pallas_call(
        join_kernel,
        in_specs=[smem] + [vmem] * size_z,
        out_shape=share_y,
        compiler_params=small,
        name="join_shares",
    )(me_z, *shares)
    total, own, place = lax.optimization_barrier((total, own, place))
    shares = gathered("gy", total)
    scalar_grad, vector_grad, positions_grad = pl.pallas_call(
        functools.partial(own_kernel, (shapes[0],)),
        out_shape=(
            jax.ShapeDtypeStruct((owned, width), f32),
            jax.ShapeDtypeStruct((owned, 3 * width), f32),
            jax.ShapeDtypeStruct((3, owned), f32),
        ),
        compiler_params=middle,
        cost_estimate=work(own, 2 * owned * 4 * width * 400),
        name="own_last",
    )(lists[0], *back_x, own, place)

    def like(x):
        return jax.ShapeDtypeStruct(x.shape, f32)

    weights = pl.pallas_call(
        functools.partial(unpack_kernel, (size_y, size_z), late_share.shape[0]),
        in_specs=[smem] + [vmem] * size_y,
        out_shape=tuple(
            like(x)
            for x in (
                message_inner,
                message_inner_bias,
                message_outer,
                message_outer_bias,
                radial_weight,
                radial_bias,
                update_left,
                update_right,
                update_inner,
                update_inner_bias,
                update_outer,
                update_outer_bias,
            )
        ),
        scratch_shapes=[
            pltpu.VMEM((late_rows, width), f32),
            pltpu.VMEM((early_rows, width), f32),
            pltpu.VMEM((late_rows + early_rows, width), f32),
        ],
        compiler_params=small,
        name="unpack_weights",
    )(me_y, *shares)
    return (out_s, out_v, scalar_grad, vector_grad, positions_grad, *weights)


def solution(mesh):
    cells = P(("gx", "gy", "gz"), None)
    columns = P(None, ("gx", "gy", "gz"))
    faces = P(("gx", "gy", "gz"), None, None)
    flat = P(("gx", "gy", "gz"))
    return jax.shard_map(
        local,
        mesh=mesh,
        in_specs=(cells, cells, columns)
        + (P(),) * 12
        + (cells, cells, faces, faces, faces, columns, flat, columns, flat),
        out_specs=(cells, cells, cells, cells, columns) + (P(),) * 12,
        check_vma=False,
    )
```

time: 3290 us -> 180 us (0.05); the launches traced: 3240 us -> 180 us
  other arithmetic: 1600 us -> 1.5 us
  local copies, waits for them, and re-layouts: 1290 us -> 2.99 us
  matrix products: 215 us -> 0 us
  Pallas kernels: 0 us -> 113 us
  blocking collectives: 46.5 us -> 0 us
  waiting for transfers between devices: 63.6 us -> 22 us
    scatter-add x126 -> x0, other arithmetic: 832 us -> none  [the longest x52 345 us: edge_backward(): grad_places.at[:, source].add(grad_offset).at[:, target].add(-grad_offset)]
    gather x180 -> x0, local copies, waits for them, and re-layouts: 591 us -> none  [the longest x52 196 us: edge_state(): jnp.take(ext_places, source, axis=1) - jnp.take(ext_places, target, axis=1)]
    reduce_sum x132 -> x0, other arithmetic: 242 us -> none  [the longest x26 73.5 us: edge_backward(): jnp.sum(grad_vector_edge * mixture[:, None, 2 * feat_width:], axis=2)]
    dot_general x122 -> x0, matrix products: 215 us -> none  [the longest x52 85.4 us: edge_state(): jnp.einsum('kn,kc->nc', radial_basis, radial_weight, preferred_element_ty...]
    mul x105 -> x0, local copies, waits for them, and re-layouts: 196 us -> none  [the longest x52 84.1 us: message_terms(): neighbour_vectors * mixture[:, None, :feat_width]]
    slice x157 -> x0, local copies, waits for them, and re-layouts: 186 us -> none  [the longest x52 63.9 us: edge_backward(): mixture[:, None, :feat_width]]
    mul x139 -> x0, other arithmetic: 127 us -> none  [the longest x26 61.6 us: edge_backward(): grad_vector_edge * mixture[:, None, :feat_width]]
    reduce_sum x78 -> x0, local copies, waits for them, and re-layouts: 117 us -> none  [the longest x26 47.7 us: edge_backward(): jnp.sum(grad_vector_edge * neighbour_vectors, axis=1)]
  transfers between devices with their start and end apart: 13 -> 26, of which waited for: 6 -> 12; matrix products, arithmetic and copies ran while one was open for 3% -> 1% of each run, Pallas kernels for 0% -> 46%
where the time goes in v1:
time: 180 us
  Pallas kernels  113 us (63%)
  starting transfers between devices  38.6 us (21%)
  waiting for transfers between devices  22 us (12%)
  local copies, waits for them, and re-layouts  2.99 us (2%)
  between operations  1.86 us (1%)
    pallas_call x1, Pallas kernels, local(): pl.pallas_call(functools.partial(backward_kernel, tuple(halo), shapes, sl...  58.6 us
    pallas_call x1, Pallas kernels, local(): pl.pallas_call(functools.partial(forward_kernel, tuple(halo), shapes, slo...  23.6 us
    pallas_call x1, Pallas kernels, local(): pl.pallas_call(functools.partial(inner_kernel, slots), in_specs=[smem] *...  15 us
    ppermute x13, starting transfers between devices, rotated(): lax.ppermute(pieces[t], axis, [(i, (i + t) % count) for i in range(count)])  12.7 us
    ppermute x13, waiting for transfers between devices, rotated(): lax.ppermute(pieces[t], axis, [(i, (i + t) % count) for i in range(count)])  12.2 us
    ppermute x4, starting transfers between devices, exchange(): lax.ppermute(packets[1], axis, up)  8.34 us
    ppermute x2, waiting for transfers between devices, exchange(): return [lax.ppermute(packets[0], axis, up)]  4.99 us
    ppermute x4, starting transfers between devices, exchange(): lax.ppermute(packets[0], axis, down)  4.42 us
  transfers between devices with their start and end apart: 26, of which 12 were waited for; matrix products, arithmetic and copies ran while one was open for 1% of the time, Pallas kernels for 46%

profile of v1, /device:TPU:1, one launch (start us, length us, event | category | flops | bytes accessed | tf_op | source)
XLA Modules:
  0.0 179.6 jit_solution(11705808061240412030)
XLA Ops:
  0.7 2.1 %pack_first.1 = (f32[208,512]{1,0:T(8,128)S(1)}, f32[1000,512]{1,0:T(8,128)S(1)}, f32[8,1000]{1,0:T(8,128)S(1)}, s32[2,120]{1,0:T(2,128)S(1)}, s32[2,144]{1,0:T(2,128)S(1)}) custom-call(s32[2,100]{1,0:T(2,128)} %bitcast.21, s32[2,120]{1,0:T(2,128)} %bitcast.29, s32[2,144]{1,0:T(2,128)} %bitcast.28, bf16[1000,128]{1,0:T(8,128)(2,1)} %s_ref.1, ...), custom_call_target="tpu_custom_call" | custom-call | tf_op jit(solution)/shard_map/pack_first/pallas_call | solution.py:232
  2.8 2.1 %collective-permute-start = (f32[208,512]{1,0:T(8,128)S(1)}, f32[208,512]{1,0:T(8,128)S(1)}, u32[]{:S(2)}, u32[]{:S(2)}) collective-permute-start(f32[208,512]{1,0:T(8,128)S(1)} %get-tuple-element.113), channel_id=1, source_target_pairs={{0,16},{16,0},{1,17},{17,1},{2,18},{18,2},{3,19},{19,3},{4,20},{20... | collective-permute-start | bytes 1277960 | tf_op jit(solution)/shard_map/ppermute | solution.py:1378
  4.9 0.8 copy-done.8
  5.7 0.7 copy-done.11
  6.4 1.8 %order_atoms.1 = (s32[16,1024]{1,0:T(8,128)S(1)}, s32[128,128]{1,0:T(8,128)S(1)}, s32[16,128]{1,0:T(8,128)S(1)}, s32[16,128]{1,0:T(8,128)S(1)}, f32[8,1024]{1,0:T(8,128)S(1)}) custom-call(s32[15,1000]{1,0:T(8,128)S(1)} %copy-done.8, s32[11,128]{1,0:T(8,128)S(1)} %copy-done.11, f32[8,1000]{1,0:T(8,128)S(1)} %get-tuple-element.105.place_ref.p_ref), custom_call_target="tpu_custom_call" | custom-call | tf_op jit(solution)/shard_map/order_atoms/pallas_call | solution.py:371
  8.2 1.2 pack_own.1
  9.4 0.0 copy-start.3
  9.4 5.0 %collective-permute-done.rest_0_ = f32[208,512]{1,0:T(8,128)S(1)} collective-permute-done((f32[208,512]{1,0:T(8,128)S(1)}, f32[208,512]{1,0:T(8,128)S(1)}, u32[]{:S(2)}, u32[]{:S(2)}) %collective-permute-start) | collective-permute-done | bytes 426016 | tf_op jit(solution)/shard_map/ppermute | solution.py:1378
  14.4 1.2 pack_rows.2
  15.6 2.6 %collective-permute-start.1 = (f32[128,512]{1,0:T(8,128)}, f32[128,512]{1,0:T(8,128)S(1)}, u32[]{:S(2)}, u32[]{:S(2)}) collective-permute-start(f32[128,512]{1,0:T(8,128)} %get-tuple-element.119), channel_id=1, source_target_pairs={{0,4},{4,8},{8,12},{12,0},{1,5},{5,9},{9,13},{13,1},{2,6},{6,10},{... | collective-permute-start | bytes 786440 | tf_op jit(solution)/shard_map/ppermute | solution.py:1380
  19.0 0.0 copy-start.2
  19.0 0.0 copy-start.5
  19.0 0.0 copy-start.13
  19.0 0.0 copy-start.16
  19.1 1.5 maximum_convert_fusion.cot_ref
  20.6 3.7 %collective-permute-done.1.rest_1_ = f32[128,512]{1,0:T(8,128)S(1)} collective-permute-done((f32[128,512]{1,0:T(8,128)}, f32[128,512]{1,0:T(8,128)S(1)}, u32[]{:S(2)}, u32[]{:S(2)}) %collective-permute-start.1) | collective-permute-done | bytes 262176 | tf_op jit(solution)/shard_map/ppermute | solution.py:1380
  24.2 0.8 collective-permute-done.2.rest_2_
  25.0 0.7 pack_rows.3
  25.7 1.6 collective-permute-start.3
  27.3 2.1 %collective-permute-start.4 = (f32[152,512]{1,0:T(8,128)S(1)}, f32[152,512]{1,0:T(8,128)S(1)}, u32[]{:S(2)}, u32[]{:S(2)}) collective-permute-start(f32[152,512]{1,0:T(8,128)S(1)} %get-tuple-element.128), channel_id=1, source_target_pairs={{1,0},{2,1},{3,2},{0,3},{5,4},{6,5},{7,6},{4,7},{9,8},{10,9},{11,1... | collective-permute-start | bytes 933896 | tf_op jit(solution)/shard_map/ppermute | solution.py:1380
  29.4 0.0 copy-start.6
  29.4 0.0 copy-start.7
  29.5 0.0 copy-start.9
  29.5 0.0 copy-start.14
  29.5 0.0 copy-start.17
  29.5 15.0 %edges_inner.1.sums_in = f32[8000,128]{1,0:T(8,128)S(1)} custom-call(s32[16384]{0:T(1024)S(1)} %bitcast.11, s32[2048]{0:T(1024)S(1)} %bitcast.14, f32[1000,512]{1,0:T(8,128)S(1)} %get-tuple-element.110.rows_ref, f32[8,1000]{1,0:T(8,128)S(1)} %get-tuple-element.105.place_ref.p_ref, s32[16,1024]{1,0:T(8,128)S(1)} %get-tuple-element.125.table_ref, ...), custom_call_target="tpu_custom_call" | custom-call | flops 6794772480 | bytes 8192000 | tf_op jit(solution)/shard_map/edges_inner/pallas_call | solution.py:1498
  44.6 23.6 %edges_forward.1 = (bf16[1000,128]{1,0:T(8,128)(2,1)}, bf16[1000,384]{1,0:T(8,128)(2,1)}, f32[8000,128]{1,0:T(8,128)S(1)}, f32[8,128]{1,0:T(8,128)S(1)}, f32[138...) custom-call(s32[16384]{0:T(1024)S(1)} %bitcast.12, ...), custom_call_target="tpu_custom_call" | custom-call | tf_op jit(solution)/shard_map/edges_forward/pallas_call | solution.py:1530
  68.2 1.9 %collective-permute-start.5 = (f32[224,128]{1,0:T(8,128)S(1)}, f32[224,128]{1,0:T(8,128)S(1)}, u32[]{:S(2)}, u32[]{:S(2)}) collective-permute-start(f32[224,128]{1,0:T(8,128)S(1)} %get-tuple-element.140), channel_id=1, source_target_pairs={{0,4},{4,8},{8,12},{12,0},{1,5},{5,9},{9,13},{13,1},{2,6},{6,10},{... | collective-permute-start | bytes 344072 | tf_op jit(solution)/shard_map/ppermute | solution.py:1386
  70.1 0.1 collective-permute-start.6
  70.3 0.8 collective-permute-start.7
  71.1 58.6 %edges_backward.1 = (f32[13824,128]{1,0:T(8,128)S(1)}, f32[9,8,128]{2,1,0:T(8,128)S(1)}, f32[640,128]{1,0:T(8,128)S(1)}, f32[104,512]{1,0:T(8,128)S(1)}, f32[104...) custom-call(s32[16384]{0:T(1024)S(1)} %bitcast.13, ...), custom_call_target="tpu_custom_call" | custom-call | flops 27179089920 | bytes 8192000 | tf_op jit(solution)/shard_map/edges_backward/pallas_call | solution.py:1590
  129.7 1.2 collective-permute-start.8
  130.9 2.3 %collective-permute-start.9 = (f32[152,512]{1,0:T(8,128)S(1)}, f32[152,512]{1,0:T(8,128)S(1)}, u32[]{:S(2)}, u32[]{:S(2)}) collective-permute-start(f32[152,512]{1,0:T(8,128)S(1)} %get-tuple-element.144), channel_id=1, source_target_pairs={{1,0},{2,1},{3,2},{0,3},{5,4},{6,5},{7,6},{4,7},{9,8},{10,9},{11,1... | collective-permute-start | bytes 933896 | tf_op jit(solution)/shard_map/ppermute | solution.py:1380
  133.3 3.3 %own_backward.1 = (f32[1000,512]{1,0:T(8,128)S(1)}, f32[8,1000]{1,0:T(8,128)S(1)}, f32[224,128]{1,0:T(8,128)S(1)}, f32[160,128]{1,0:T(8,128)S(1)}, f32[160,128]{...) custom-call(s32[1]{0:T(128)} %bitcast.6.place_y.me, f32[13824,128]{1,0:T(8,128)S(1)} %get-tuple-element.145.sums, ...), custom_call_target="tpu_custom_call" | custom-call | tf_op jit(solution)/shard_map/own_backward/pallas_call | solution.py:1638
  136.5 1.3 copy-done.18
  137.9 1.5 collective-permute-start.10
  139.4 1.3 collective-permute-start.11
  140.7 0.1 collective-permute-start.12
  140.8 0.1 collective-permute-done.10.refs_3_
  140.9 4.0 %collective-permute-done.11.refs_4_ = f32[160,128]{1,0:T(8,128)S(1)} collective-permute-done((f32[160,128]{1,0:T(8,128)S(1)}, f32[160,128]{1,0:T(8,128)S(1)}, u32[]{:S(2)}, u32[]{:S(2)}) %collective-permute-start.11) | collective-permute-done | bytes 81952 | tf_op jit(solution)/shard_map/ppermute | solution.py:1386
  144.9 0.6 collective-permute-done.12.refs_5_
  145.5 0.2 collective-permute-done.9.refs_1_.refs_3_
  145.7 0.4 return_y.1
  146.1 2.9 %collective-permute-start.13 = (f32[128,512]{1,0:T(8,128)S(1)}, f32[128,512]{1,0:T(8,128)S(1)}, u32[]{:S(2)}, u32[]{:S(2)}) collective-permute-start(f32[128,512]{1,0:T(8,128)S(1)} %get-tuple-element.159), channel_id=1, source_target_pairs={{0,4},{4,8},{8,12},{12,0},{1,5},{5,9},{9,13},{13,1},{2,6},{6,10},{... | collective-permute-start | bytes 786440 | tf_op jit(solution)/shard_map/ppermute | solution.py:1380
  149.0 0.8 collective-permute-start.15
  149.8 1.4 collective-permute-start.16
  151.2 1.3 collective-permute-start.17
  152.5 1.3 collective-permute-done.15.refs_5_
  153.8 2.6 %collective-permute-done.16.refs_6_ = f32[96,128]{1,0:T(8,128)S(1)} collective-permute-done((f32[96,128]{1,0:T(8,128)S(1)}, f32[96,128]{1,0:T(8,128)S(1)}, u32[]{:S(2)}, u32[]{:S(2)}) %collective-permute-start.16) | collective-permute-done | bytes 49184 | tf_op jit(solution)/shard_map/ppermute | solution.py:1386
  156.4 0.5 return_x.1
  156.9 0.7 collective-permute-start.18
  157.6 2.3 %collective-permute-done.18.refs_1_ = f32[96,128]{1,0:T(8,128)S(1)} collective-permute-done((f32[96,128]{1,0:T(8,128)S(1)}, f32[96,128]{1,0:T(8,128)S(1)}, u32[]{:S(2)}, u32[]{:S(2)}) %collective-permute-start.18) | collective-permute-done | bytes 49184 | tf_op jit(solution)/shard_map/ppermute | solution.py:1386
  159.9 1.7 collective-permute-start.22
  161.6 0.9 collective-permute-start.21
  162.5 0.1 collective-permute-start.20
  162.6 2.0 %collective-permute-start.19 = (f32[208,512]{1,0:T(8,128)S(1)}, f32[208,512]{1,0:T(8,128)S(1)}, u32[]{:S(2)}, u32[]{:S(2)}) collective-permute-start(f32[208,512]{1,0:T(8,128)S(1)} %get-tuple-element.169), channel_id=1, source_target_pairs={{0,16},{16,0},{1,17},{17,1},{2,18},{18,2},{3,19},{19,3},{4,20},{20... | collective-permute-start | bytes 1277960 | tf_op jit(solution)/shard_map/ppermute | solution.py:1378
  164.6 1.4 own_partial.1
  166.1 1.4 collective-permute-done.20.refs_1_
  167.5 0.5 collective-permute-start.24
  168.0 4.3 %collective-permute-start.23 = (f32[384,128]{1,0:T(8,128)S(1)}, f32[384,128]{1,0:T(8,128)S(1)}, u32[]{:S(2)}, u32[]{:S(2)}) collective-permute-start(f32[384,128]{1,0:T(8,128)S(1)} %join_shares.1.refs_0_), channel_id=1, source_target_pairs={{0,4},{4,0},{8,12},{12,8},{1,5},{5,1},{9,13},{13,9},{2,6},{6,2},{1... | collective-permute-start | bytes 589832 | tf_op jit(solution)/shard_map/ppermute | solution.py:1396
  172.2 0.1 collective-permute-done.24.refs_2_
  172.3 4.3 %collective-permute-start.25 = (f32[384,128]{1,0:T(8,128)S(1)}, f32[384,128]{1,0:T(8,128)S(1)}, u32[]{:S(2)}, u32[]{:S(2)}) collective-permute-start(f32[384,128]{1,0:T(8,128)S(1)} %collective-permute-done.24.refs_2_), channel_id=1, source_target_pairs={{0,4},{4,0},{8,12},{12,8},{1,5},{5,1},{9,13},{13,9},{2,6},{6,2},{1... | collective-permute-start | bytes 589832 | tf_op jit(solution)/shard_map/ppermute | solution.py:1397
  176.6 1.9 %own_last.1 = (f32[1000,128]{1,0:T(8,128)}, f32[1000,384]{1,0:T(8,128)}, f32[3,1000]{1,0:T(4,128)}) custom-call(s32[2,100]{1,0:T(2,128)S(1)} %bitcast.22, f32[208,512]{1,0:T(8,128)S(1)} %collective-permute-done.19.refs_1_, f32[1000,512]{1,0:T(8,128)S(1)} %get-tuple-element.175.refs_2_, f32[8,1000]{1,0:T(8,128)S(1)} %get-tuple-element.176.refs_3_), custom_call_target="tpu_custom_call" | custom-call | flops 409600000 | bytes 8192000 | tf_op jit(solution)/shard_map/own_last/pallas_call | solution.py:1700
  178.6 0.9 unpack_weights.1
  (54 shorter events, 0.1 us)
Async XLA Ops:
  0.7 18.3 %copy-start.20 = (f32[384]{0:T(512)S(1)}, f32[384]{0:T(512)}, u32[]{:S(2)}) copy-start(f32[384]{0:T(512)} %param.30) | copy-start | bytes 4612
  0.7 18.3 %copy-start.21 = (f32[384]{0:T(512)S(1)}, f32[384]{0:T(512)}, u32[]{:S(2)}) copy-start(f32[384]{0:T(512)} %param.32) | copy-start | bytes 4612
  0.7 18.3 %copy-start.22 = (f32[384]{0:T(512)S(1)}, f32[384]{0:T(512)}, u32[]{:S(2)}) copy-start(f32[384]{0:T(512)} %param.38) | copy-start | bytes 4612
  2.8 11.6 %collective-permute-start = (f32[208,512]{1,0:T(8,128)S(1)}, f32[208,512]{1,0:T(8,128)S(1)}, u32[]{:S(2)}, u32[]{:S(2)}) collective-permute-start(f32[208,512]{1,0:T(8,128)S(1)} %get-tuple-element.113), channel_id=1, source_target_pairs={{0,16},{16,0},{1,17},{17,1},{2,18},{18,2},{3,19},{19,3},{4,20},{20... | collective-permute-start | bytes 1277960 | tf_op jit(solution)/shard_map/ppermute | solution.py:1378
  4.9 0.8 copy-start.8
  5.7 0.7 copy-start.11
  9.4 6.2 %copy-start.3 = (f32[152,512]{1,0:T(8,128)}, f32[152,512]{1,0:T(8,128)S(1)}, u32[]{:S(2)}) copy-start(f32[152,512]{1,0:T(8,128)S(1)} %get-tuple-element.112.own_upper) | copy-start | bytes 933892
  15.6 8.6 %collective-permute-start.1 = (f32[128,512]{1,0:T(8,128)}, f32[128,512]{1,0:T(8,128)S(1)}, u32[]{:S(2)}, u32[]{:S(2)}) collective-permute-start(f32[128,512]{1,0:T(8,128)} %get-tuple-element.119), channel_id=1, source_target_pairs={{0,4},{4,8},{8,12},{12,0},{1,5},{5,9},{9,13},{13,1},{2,6},{6,10},{... | collective-permute-start | bytes 786440 | tf_op jit(solution)/shard_map/ppermute | solution.py:1380
  18.2 6.7 %collective-permute-start.2 = (f32[128,512]{1,0:T(8,128)}, f32[128,512]{1,0:T(8,128)S(1)}, u32[]{:S(2)}, u32[]{:S(2)}) collective-permute-start(f32[128,512]{1,0:T(8,128)} %get-tuple-element.120), channel_id=1, source_target_pairs={{4,0},{8,4},{12,8},{0,12},{5,1},{9,5},{13,9},{1,13},{6,2},{10,6},{... | collective-permute-start | bytes 786440 | tf_op jit(solution)/shard_map/ppermute | solution.py:1380
  18.2 6.7 %copy-start.4 = (f32[152,512]{1,0:T(8,128)S(1)}, f32[152,512]{1,0:T(8,128)}, u32[]{:S(2)}) copy-start(f32[152,512]{1,0:T(8,128)} %copy-done.3) | copy-start | bytes 933892
  19.0 10.4 %copy-start.2 = (bf16[128,384]{1,0:T(8,128)(2,1)S(1)}, bf16[128,384]{1,0:T(8,128)(2,1)}, u32[]{:S(2)}) copy-start(bf16[128,384]{1,0:T(8,128)(2,1)} %w2_ref.7) | copy-start | bytes 294916
  19.0 10.4 %copy-start.5 = (bf16[128,128]{1,0:T(8,128)(2,1)S(1)}, bf16[128,128]{1,0:T(8,128)(2,1)}, u32[]{:S(2)}) copy-start(bf16[128,128]{1,0:T(8,128)(2,1)} %w1_ref.7) | copy-start | bytes 98308
  19.0 10.4 %copy-start.13 = (bf16[20,384]{1,0:T(8,128)(2,1)S(1)}, bf16[20,384]{1,0:T(8,128)(2,1)}, u32[]{:S(2)}) copy-start(bf16[20,384]{1,0:T(8,128)(2,1)} %wr_ref.5) | copy-start | bytes 46084
  19.0 10.4 %copy-start.16 = (f32[128]{0:T(128)S(1)}, f32[128]{0:T(128)}, u32[]{:S(2)}) copy-start(f32[128]{0:T(128)} %param.28) | copy-start | bytes 1540
  25.7 18.8 %collective-permute-start.3 = (f32[152,512]{1,0:T(8,128)S(1)}, f32[152,512]{1,0:T(8,128)S(1)}, u32[]{:S(2)}, u32[]{:S(2)}) collective-permute-start(f32[152,512]{1,0:T(8,128)S(1)} %get-tuple-element.127), channel_id=1, source_target_pairs={{0,1},{1,2},{2,3},{3,0},{4,5},{5,6},{6,7},{7,4},{8,9},{9,10},{10,1... | collective-permute-start | bytes 933896 | tf_op jit(solution)/shard_map/ppermute | solution.py:1380
  27.3 17.2 %collective-permute-start.4 = (f32[152,512]{1,0:T(8,128)S(1)}, f32[152,512]{1,0:T(8,128)S(1)}, u32[]{:S(2)}, u32[]{:S(2)}) collective-permute-start(f32[152,512]{1,0:T(8,128)S(1)} %get-tuple-element.128), channel_id=1, source_target_pairs={{1,0},{2,1},{3,2},{0,3},{5,4},{6,5},{7,6},{4,7},{9,8},{10,9},{11,1... | collective-permute-start | bytes 933896 | tf_op jit(solution)/shard_map/ppermute | solution.py:1380
  29.4 15.1 %copy-start.6 = (bf16[128,384]{1,0:T(8,128)(2,1)S(1)}, bf16[128,384]{1,0:T(8,128)(2,1)}, u32[]{:S(2)}) copy-start(bf16[128,384]{1,0:T(8,128)(2,1)} %w4_ref.1) | copy-start | bytes 294916
  29.4 15.1 %copy-start.7 = (bf16[256,128]{1,0:T(8,128)(2,1)S(1)}, bf16[256,128]{1,0:T(8,128)(2,1)}, u32[]{:S(2)}) copy-start(bf16[256,128]{1,0:T(8,128)(2,1)} %w3_ref.1) | copy-start | bytes 196612
  29.5 15.1 %copy-start.9 = (bf16[128,128]{1,0:T(8,128)(2,1)S(1)}, bf16[128,128]{1,0:T(8,128)(2,1)}, u32[]{:S(2)}) copy-start(bf16[128,128]{1,0:T(8,128)(2,1)} %u_ref.1) | copy-start | bytes 98308
  29.5 15.1 %copy-start.10 = (bf16[128,128]{1,0:T(8,128)(2,1)S(1)}, bf16[128,128]{1,0:T(8,128)(2,1)}, u32[]{:S(2)}) copy-start(bf16[128,128]{1,0:T(8,128)(2,1)} %v_ref.2) | copy-start | bytes 98308
  29.5 15.1 %copy-start.12 = (s32[11,128]{1,0:T(8,128)S(1)}, s32[11,128]{1,0:T(8,128)}, u32[]{:S(2)}) copy-start(s32[11,128]{1,0:T(8,128)} %hub_table_ref.3) | copy-start | bytes 16900
  29.5 15.1 %copy-start.14 = (s32[128]{0:T(128)S(1)}, s32[128]{0:T(128)}, u32[]{:S(2)}) copy-start(s32[128]{0:T(128)} %hub_list.3) | copy-start | bytes 1540
  29.5 15.1 %copy-start.17 = (f32[128]{0:T(128)S(1)}, f32[128]{0:T(128)}, u32[]{:S(2)}) copy-start(f32[128]{0:T(128)} %param.36) | copy-start | bytes 1540
  68.2 61.5 %collective-permute-start.5 = (f32[224,128]{1,0:T(8,128)S(1)}, f32[224,128]{1,0:T(8,128)S(1)}, u32[]{:S(2)}, u32[]{:S(2)}) collective-permute-start(f32[224,128]{1,0:T(8,128)S(1)} %get-tuple-element.140), channel_id=1, source_target_pairs={{0,4},{4,8},{8,12},{12,0},{1,5},{5,9},{9,13},{13,1},{2,6},{6,10},{... | collective-permute-start | bytes 344072 | tf_op jit(solution)/shard_map/ppermute | solution.py:1386
  70.1 59.6 %collective-permute-start.6 = (f32[224,128]{1,0:T(8,128)S(1)}, f32[224,128]{1,0:T(8,128)S(1)}, u32[]{:S(2)}, u32[]{:S(2)}) collective-permute-start(f32[224,128]{1,0:T(8,128)S(1)} %get-tuple-element.141), channel_id=1, source_target_pairs={{0,8},{4,12},{8,0},{12,4},{1,9},{5,13},{9,1},{13,5},{2,10},{6,14},... | collective-permute-start | bytes 344072 | tf_op jit(solution)/shard_map/ppermute | solution.py:1386
  70.3 59.4 %collective-permute-start.7 = (f32[224,128]{1,0:T(8,128)S(1)}, f32[224,128]{1,0:T(8,128)S(1)}, u32[]{:S(2)}, u32[]{:S(2)}) collective-permute-start(f32[224,128]{1,0:T(8,128)S(1)} %get-tuple-element.142), channel_id=1, source_target_pairs={{0,12},{4,0},{8,4},{12,8},{1,13},{5,1},{9,5},{13,9},{2,14},{6,2},{... | collective-permute-start | bytes 344072 | tf_op jit(solution)/shard_map/ppermute | solution.py:1386
  71.1 62.2 %copy-start = (bf16[1000,384]{1,0:T(8,128)(2,1)S(1)}, bf16[1000,384]{1,0:T(8,128)(2,1)}, u32[]{:S(2)}) copy-start(bf16[1000,384]{1,0:T(8,128)(2,1)} %v_ref.3) | copy-start | bytes 2304004
  71.1 62.2 %copy-start.1 = (bf16[1000,128]{1,0:T(8,128)(2,1)S(1)}, bf16[1000,128]{1,0:T(8,128)(2,1)}, u32[]{:S(2)}) copy-start(bf16[1000,128]{1,0:T(8,128)(2,1)} %s_ref.1) | copy-start | bytes 768004
  129.7 15.8 %collective-permute-start.8 = (f32[152,512]{1,0:T(8,128)}, f32[152,512]{1,0:T(8,128)S(1)}, u32[]{:S(2)}, u32[]{:S(2)}) collective-permute-start(f32[152,512]{1,0:T(8,128)} %get-tuple-element.143), channel_id=1, source_target_pairs={{0,1},{1,2},{2,3},{3,0},{4,5},{5,6},{6,7},{7,4},{8,9},{9,10},{10,1... | collective-permute-start | bytes 933896 | tf_op jit(solution)/shard_map/ppermute | solution.py:1380
  130.9 14.8 %collective-permute-start.9 = (f32[152,512]{1,0:T(8,128)S(1)}, f32[152,512]{1,0:T(8,128)S(1)}, u32[]{:S(2)}, u32[]{:S(2)}) collective-permute-start(f32[152,512]{1,0:T(8,128)S(1)} %get-tuple-element.144), channel_id=1, source_target_pairs={{1,0},{2,1},{3,2},{0,3},{5,4},{6,5},{7,6},{4,7},{9,8},{10,9},{11,1... | collective-permute-start | bytes 933896 | tf_op jit(solution)/shard_map/ppermute | solution.py:1380
  136.5 1.4 copy-start.18
  137.9 3.0 %collective-permute-start.10 = (f32[160,128]{1,0:T(8,128)S(1)}, f32[160,128]{1,0:T(8,128)S(1)}, u32[]{:S(2)}, u32[]{:S(2)}) collective-permute-start(f32[160,128]{1,0:T(8,128)S(1)} %get-tuple-element.153), channel_id=1, source_target_pairs={{0,4},{4,8},{8,12},{12,0},{1,5},{5,9},{9,13},{13,1},{2,6},{6,10},{... | collective-permute-start | bytes 245768 | tf_op jit(solution)/shard_map/ppermute | solution.py:1386
  139.4 5.5 %collective-permute-start.11 = (f32[160,128]{1,0:T(8,128)S(1)}, f32[160,128]{1,0:T(8,128)S(1)}, u32[]{:S(2)}, u32[]{:S(2)}) collective-permute-start(f32[160,128]{1,0:T(8,128)S(1)} %get-tuple-element.154), channel_id=1, source_target_pairs={{0,8},{4,12},{8,0},{12,4},{1,9},{5,13},{9,1},{13,5},{2,10},{6,14},... | collective-permute-start | bytes 245768 | tf_op jit(solution)/shard_map/ppermute | solution.py:1386
  140.7 4.8 %collective-permute-start.12 = (f32[160,128]{1,0:T(8,128)S(1)}, f32[160,128]{1,0:T(8,128)S(1)}, u32[]{:S(2)}, u32[]{:S(2)}) collective-permute-start(f32[160,128]{1,0:T(8,128)S(1)} %get-tuple-element.155), channel_id=1, source_target_pairs={{0,12},{4,0},{8,4},{12,8},{1,13},{5,1},{9,5},{13,9},{2,14},{6,2},{... | collective-permute-start | bytes 245768 | tf_op jit(solution)/shard_map/ppermute | solution.py:1386
  140.8 23.8 %copy-start.19 = (f32[1000,512]{1,0:T(8,128)S(1)}, f32[1000,512]{1,0:T(8,128)}, u32[]{:S(2)}) copy-start(f32[1000,512]{1,0:T(8,128)} %copy-done.18) | copy-start | bytes 6144004
  146.1 10.3 %collective-permute-start.13 = (f32[128,512]{1,0:T(8,128)S(1)}, f32[128,512]{1,0:T(8,128)S(1)}, u32[]{:S(2)}, u32[]{:S(2)}) collective-permute-start(f32[128,512]{1,0:T(8,128)S(1)} %get-tuple-element.159), channel_id=1, source_target_pairs={{0,4},{4,8},{8,12},{12,0},{1,5},{5,9},{9,13},{13,1},{2,6},{6,10},{... | collective-permute-start | bytes 786440 | tf_op jit(solution)/shard_map/ppermute | solution.py:1380
  149.0 7.4 %collective-permute-start.14 = (f32[128,512]{1,0:T(8,128)S(1)}, f32[128,512]{1,0:T(8,128)S(1)}, u32[]{:S(2)}, u32[]{:S(2)}) collective-permute-start(f32[128,512]{1,0:T(8,128)S(1)} %get-tuple-element.160), channel_id=1, source_target_pairs={{4,0},{8,4},{12,8},{0,12},{5,1},{9,5},{13,9},{1,13},{6,2},{10,6},{... | collective-permute-start | bytes 786440 | tf_op jit(solution)/shard_map/ppermute | solution.py:1380
  149.0 4.9 %collective-permute-start.15 = (f32[96,128]{1,0:T(8,128)S(1)}, f32[96,128]{1,0:T(8,128)S(1)}, u32[]{:S(2)}, u32[]{:S(2)}) collective-permute-start(f32[96,128]{1,0:T(8,128)S(1)} %get-tuple-element.162), channel_id=1, source_target_pairs={{0,1},{1,2},{2,3},{3,0},{4,5},{5,6},{6,7},{7,4},{8,9},{9,10},{10,1... | collective-permute-start | bytes 147464 | tf_op jit(solution)/shard_map/ppermute | solution.py:1386
  149.8 6.6 %collective-permute-start.16 = (f32[96,128]{1,0:T(8,128)S(1)}, f32[96,128]{1,0:T(8,128)S(1)}, u32[]{:S(2)}, u32[]{:S(2)}) collective-permute-start(f32[96,128]{1,0:T(8,128)S(1)} %get-tuple-element.163), channel_id=1, source_target_pairs={{0,2},{1,3},{2,0},{3,1},{4,6},{5,7},{6,4},{7,5},{8,10},{9,11},{10,... | collective-permute-start | bytes 147464 | tf_op jit(solution)/shard_map/ppermute | solution.py:1386
  151.2 5.2 %collective-permute-start.17 = (f32[96,128]{1,0:T(8,128)S(1)}, f32[96,128]{1,0:T(8,128)S(1)}, u32[]{:S(2)}, u32[]{:S(2)}) collective-permute-start(f32[96,128]{1,0:T(8,128)S(1)} %get-tuple-element.164), channel_id=1, source_target_pairs={{0,3},{1,0},{2,1},{3,2},{4,7},{5,4},{6,5},{7,6},{8,11},{9,8},{10,9... | collective-permute-start | bytes 147464 | tf_op jit(solution)/shard_map/ppermute | solution.py:1386
  156.9 3.0 %collective-permute-start.18 = (f32[96,128]{1,0:T(8,128)S(1)}, f32[96,128]{1,0:T(8,128)S(1)}, u32[]{:S(2)}, u32[]{:S(2)}) collective-permute-start(f32[96,128]{1,0:T(8,128)S(1)} %get-tuple-element.168.refs_0_), channel_id=1, source_target_pairs={{0,16},{16,0},{1,17},{17,1},{2,18},{18,2},{3,19},{19,3},{4,20},{20... | collective-permute-start | bytes 147464 | tf_op jit(solution)/shard_map/ppermute | solution.py:1386
  159.9 6.1 %collective-permute-start.22 = (f32[96,128]{1,0:T(8,128)S(1)}, f32[96,128]{1,0:T(8,128)S(1)}, u32[]{:S(2)}, u32[]{:S(2)}) collective-permute-start(f32[96,128]{1,0:T(8,128)S(1)} %sum_last.1.refs_0_), channel_id=1, source_target_pairs={{0,3},{1,0},{2,1},{3,2},{4,7},{5,4},{6,5},{7,6},{8,11},{9,8},{10,9... | collective-permute-start | bytes 147464 | tf_op jit(solution)/shard_map/ppermute | solution.py:1386
  161.6 4.5 %collective-permute-start.21 = (f32[96,128]{1,0:T(8,128)S(1)}, f32[96,128]{1,0:T(8,128)S(1)}, u32[]{:S(2)}, u32[]{:S(2)}) collective-permute-start(f32[96,128]{1,0:T(8,128)S(1)} %sum_last.1.refs_0_), channel_id=1, source_target_pairs={{0,2},{1,3},{2,0},{3,1},{4,6},{5,7},{6,4},{7,5},{8,10},{9,11},{10,... | collective-permute-start | bytes 147464 | tf_op jit(solution)/shard_map/ppermute | solution.py:1386
  162.5 5.0 %collective-permute-start.20 = (f32[96,128]{1,0:T(8,128)S(1)}, f32[96,128]{1,0:T(8,128)S(1)}, u32[]{:S(2)}, u32[]{:S(2)}) collective-permute-start(f32[96,128]{1,0:T(8,128)S(1)} %sum_last.1.refs_0_), channel_id=1, source_target_pairs={{0,1},{1,2},{2,3},{3,0},{4,5},{5,6},{6,7},{7,4},{8,9},{9,10},{10,1... | collective-permute-start | bytes 147464 | tf_op jit(solution)/shard_map/ppermute | solution.py:1386
  162.6 14.0 %collective-permute-start.19 = (f32[208,512]{1,0:T(8,128)S(1)}, f32[208,512]{1,0:T(8,128)S(1)}, u32[]{:S(2)}, u32[]{:S(2)}) collective-permute-start(f32[208,512]{1,0:T(8,128)S(1)} %get-tuple-element.169), channel_id=1, source_target_pairs={{0,16},{16,0},{1,17},{17,1},{2,18},{18,2},{3,19},{19,3},{4,20},{20... | collective-permute-start | bytes 1277960 | tf_op jit(solution)/shard_map/ppermute | solution.py:1378
  164.6 12.0 %copy-start.15 = (s32[1,2,100]{2,1,0:T(2,128)S(1)}, s32[1,2,100]{2,1,0:T(2,128)}, u32[]{:S(2)}) copy-start(s32[1,2,100]{2,1,0:T(2,128)} %param.41) | copy-start | bytes 2404
  167.5 4.9 %collective-permute-start.24 = (f32[384,128]{1,0:T(8,128)S(1)}, f32[384,128]{1,0:T(8,128)S(1)}, u32[]{:S(2)}, u32[]{:S(2)}) collective-permute-start(f32[384,128]{1,0:T(8,128)S(1)} %join_shares.1.refs_0_), channel_id=1, source_target_pairs={{0,8},{4,12},{8,0},{12,4},{1,9},{5,13},{9,1},{13,5},{2,10},{6,14},... | collective-permute-start | bytes 589832 | tf_op jit(solution)/shard_map/ppermute | solution.py:1395
  168.0 10.6 %collective-permute-start.23 = (f32[384,128]{1,0:T(8,128)S(1)}, f32[384,128]{1,0:T(8,128)S(1)}, u32[]{:S(2)}, u32[]{:S(2)}) collective-permute-start(f32[384,128]{1,0:T(8,128)S(1)} %join_shares.1.refs_0_), channel_id=1, source_target_pairs={{0,4},{4,0},{8,12},{12,8},{1,5},{5,1},{9,13},{13,9},{2,6},{6,2},{1... | collective-permute-start | bytes 589832 | tf_op jit(solution)/shard_map/ppermute | solution.py:1396
  172.3 6.2 %collective-permute-start.25 = (f32[384,128]{1,0:T(8,128)S(1)}, f32[384,128]{1,0:T(8,128)S(1)}, u32[]{:S(2)}, u32[]{:S(2)}) collective-permute-start(f32[384,128]{1,0:T(8,128)S(1)} %collective-permute-done.24.refs_2_), channel_id=1, source_target_pairs={{0,4},{4,0},{8,12},{12,8},{1,5},{5,1},{9,13},{13,9},{2,6},{6,2},{1... | collective-permute-start | bytes 589832 | tf_op jit(solution)/shard_map/ppermute | solution.py:1397

commit v2 on v1

--- a/solution.py
+++ b/solution.py
@@ -18,7 +18,6 @@
 SLOTS = 16
 ORDER_ROWS = 24
 GROUP = 3
-PARTS = 4
 MIB = 1024 * 1024
 f32 = jnp.float32
 bf16 = jnp.bfloat16
@@ -793,13 +792,19 @@
             sum_group(filt, tiles, flat_table, targets, sums, b, i, listed)
             return inner
 
+        def pairs(i, inner):
+            for part in range(2):
+                sum_group(filt, tiles, flat_table, targets, sums, b, 2 * i + part, listed)
+            return inner
+
         start = jnp.maximum(done - b * each, 0)
-        lax.fori_loop(start, jnp.minimum(each, owned // TILE - b * each), atoms, 0)
+        end = jnp.minimum(each, owned // TILE - b * each)
+        lax.fori_loop(start // 2, end // 2, pairs, 0)
+        lax.fori_loop(end // 2 * 2, end, atoms, 0)
         return carry
 
     lax.fori_loop(done // each, blocks, regular_block, 0)
-    hub_span = min(listed, up_to(hub_listed, 4))
-    make_filters(blocks, hub_span, rows, basis_sc, geo_sc, wext, filt, width)
+    make_filters(blocks, min(listed, up_to(hub_listed, 4)), rows, basis_sc, geo_sc, wext, filt, width)
 
     def hub_slots(i, carry):
         for n in range(TILE):
@@ -986,8 +991,8 @@
 
     def block_grads(b, count, trips, source_of, target_of):
         def mixes(pair, inner):
-            for part in range(PARTS):
-                i = pair * PARTS + part
+            for part in range(2):
+                i = pair * 2 + part
                 for n in range(TILE):
                     grad = source_at(grads, target_of(i, n))
                     for k in range(count):
@@ -1075,8 +1080,8 @@
         )
 
         def scatter(pair, inner):
-            for part in range(PARTS):
-                i = pair * PARTS + part
+            for part in range(2):
+                i = pair * 2 + part
                 for n in range(TILE):
                     grad = source_at(grads, target_of(i, n))
                     places = [
@@ -1098,7 +1103,7 @@
         block_grads(
             b,
             listed,
-            (jnp.minimum(LANES, owned - base) + PARTS * TILE - 1) // (PARTS * TILE),
+            (jnp.minimum(LANES, owned - base) + 2 * TILE - 1) // (2 * TILE),
             lambda i, k, n: flat_table[(base + i * TILE) * SLOTS + k * TILE + n],
             lambda i, n: targets[base + i * TILE + n],
         )
@@ -1108,7 +1113,7 @@
     block_grads(
         blocks,
         hub_listed,
-        (hub_live + PARTS * TILE - 1) // (PARTS * TILE),
+        (hub_live + 2 * TILE - 1) // (2 * TILE),
         lambda i, k, n: flat_hub_table[i * LANES + k * TILE + n],
         lambda i, n: hub_list[i * TILE + n] * TILE,
     )

time: 180 us -> 180 us (level)
  starting transfers between devices: 38.6 us -> 41.9 us
  waiting for transfers between devices: 22 us -> 18.9 us
    ppermute x13, starting transfers between devices: 12.7 us -> 16.7 us  [rotated(): lax.ppermute(pieces[t], axis, [(i, (i + t) % count) for i in range(count)])]
    ppermute x13, waiting for transfers between devices: 12.2 us -> 9.52 us  [rotated(): lax.ppermute(pieces[t], axis, [(i, (i + t) % count) for i in range(count)])]
    ppermute x4, starting transfers between devices: 8.34 us -> 5.9 us  [exchange(): lax.ppermute(packets[1], axis, up)]
  transfers between devices with their start and end apart: 26 -> 26, of which waited for: 12 -> 11; matrix products, arithmetic and copies ran while one was open for 1% -> 1% of each run, Pallas kernels for 46% -> 46%
where the time goes in v2:
time: 180 us; the launch traced here: 179 us
  Pallas kernels  112 us (62%)
  starting transfers between devices  41.9 us (23%)
  waiting for transfers between devices  18.9 us (10%)
  local copies, waits for them, and re-layouts  2.99 us (2%)
  between operations  1.86 us (1%)
    pallas_call x1, Pallas kernels, local(): pl.pallas_call(functools.partial(backward_kernel, tuple(halo), shapes, sl...  58.5 us
    pallas_call x1, Pallas kernels, local(): pl.pallas_call(functools.partial(forward_kernel, tuple(halo), shapes, slo...  23.2 us
    ppermute x13, starting transfers between devices, rotated(): lax.ppermute(pieces[t], axis, [(i, (i + t) % count) for i in range(count)])  16.7 us
    pallas_call x1, Pallas kernels, local(): pl.pallas_call(functools.partial(inner_kernel, slots), in_specs=[smem] *...  15 us
    ppermute x13, waiting for transfers between devices, rotated(): lax.ppermute(pieces[t], axis, [(i, (i + t) % count) for i in range(count)])  9.52 us
    ppermute x4, starting transfers between devices, exchange(): lax.ppermute(packets[1], axis, up)  5.9 us
    ppermute x1, starting transfers between devices, gathered(): near = lax.ppermute(piece, axis, beside)  5.43 us
    ppermute x4, starting transfers between devices, exchange(): lax.ppermute(packets[0], axis, down)  5.34 us
  transfers between devices with their start and end apart: 26, of which 11 were waited for; matrix products, arithmetic and copies ran while one was open for 1% of the time, Pallas kernels for 46%

profile of v2, /device:TPU:1, one launch (start us, length us, event | category | flops | bytes accessed | tf_op | source)
XLA Modules:
  0.0 179.4 jit_solution(4979807591532988954)
XLA Ops:
  0.7 2.1 %pack_first.1 = (f32[208,512]{1,0:T(8,128)S(1)}, f32[1000,512]{1,0:T(8,128)S(1)}, f32[8,1000]{1,0:T(8,128)S(1)}, s32[2,120]{1,0:T(2,128)S(1)}, s32[2,144]{1,0:T(2,128)S(1)}) custom-call(s32[2,100]{1,0:T(2,128)} %bitcast.21, s32[2,120]{1,0:T(2,128)} %bitcast.29, s32[2,144]{1,0:T(2,128)} %bitcast.28, bf16[1000,128]{1,0:T(8,128)(2,1)} %s_ref.1, ...), custom_call_target="tpu_custom_call" | custom-call | tf_op jit(solution)/shard_map/pack_first/pallas_call | solution.py:231
  2.8 2.1 %collective-permute-start = (f32[208,512]{1,0:T(8,128)S(1)}, f32[208,512]{1,0:T(8,128)S(1)}, u32[]{:S(2)}, u32[]{:S(2)}) collective-permute-start(f32[208,512]{1,0:T(8,128)S(1)} %get-tuple-element.113), channel_id=1, source_target_pairs={{0,16},{16,0},{1,17},{17,1},{2,18},{18,2},{3,19},{19,3},{4,20},{20... | collective-permute-start | bytes 1277960 | tf_op jit(solution)/shard_map/ppermute | solution.py:1383
  4.9 0.8 copy-done.8
  5.7 0.7 copy-done.11
  6.4 1.8 %order_atoms.1 = (s32[16,1024]{1,0:T(8,128)S(1)}, s32[128,128]{1,0:T(8,128)S(1)}, s32[16,128]{1,0:T(8,128)S(1)}, s32[16,128]{1,0:T(8,128)S(1)}, f32[8,1024]{1,0:T(8,128)S(1)}) custom-call(s32[15,1000]{1,0:T(8,128)S(1)} %copy-done.8, s32[11,128]{1,0:T(8,128)S(1)} %copy-done.11, f32[8,1000]{1,0:T(8,128)S(1)} %get-tuple-element.105.place_ref.p_ref), custom_call_target="tpu_custom_call" | custom-call | tf_op jit(solution)/shard_map/order_atoms/pallas_call | solution.py:370
  8.2 1.2 pack_own.1
  9.4 0.0 copy-start.3
  9.4 5.0 %collective-permute-done.rest_0_ = f32[208,512]{1,0:T(8,128)S(1)} collective-permute-done((f32[208,512]{1,0:T(8,128)S(1)}, f32[208,512]{1,0:T(8,128)S(1)}, u32[]{:S(2)}, u32[]{:S(2)}) %collective-permute-start) | collective-permute-done | bytes 426016 | tf_op jit(solution)/shard_map/ppermute | solution.py:1383
  14.4 1.2 pack_rows.2
  15.6 2.6 %collective-permute-start.1 = (f32[128,512]{1,0:T(8,128)}, f32[128,512]{1,0:T(8,128)S(1)}, u32[]{:S(2)}, u32[]{:S(2)}) collective-permute-start(f32[128,512]{1,0:T(8,128)} %get-tuple-element.119), channel_id=1, source_target_pairs={{0,4},{4,8},{8,12},{12,0},{1,5},{5,9},{9,13},{13,1},{2,6},{6,10},{... | collective-permute-start | bytes 786440 | tf_op jit(solution)/shard_map/ppermute | solution.py:1385
  18.2 0.0 collective-permute-start.2
  19.0 0.0 copy-start.2
  19.0 0.0 copy-start.5
  19.0 0.0 copy-start.13
  19.0 0.0 copy-start.16
  19.1 1.5 maximum_convert_fusion.cot_ref
  20.6 3.7 %collective-permute-done.1.rest_1_ = f32[128,512]{1,0:T(8,128)S(1)} collective-permute-done((f32[128,512]{1,0:T(8,128)}, f32[128,512]{1,0:T(8,128)S(1)}, u32[]{:S(2)}, u32[]{:S(2)}) %collective-permute-start.1) | collective-permute-done | bytes 262176 | tf_op jit(solution)/shard_map/ppermute | solution.py:1385
  24.2 0.8 collective-permute-done.2.rest_2_
  25.0 0.7 pack_rows.3
  25.7 1.6 collective-permute-start.3
  27.3 2.1 %collective-permute-start.4 = (f32[152,512]{1,0:T(8,128)S(1)}, f32[152,512]{1,0:T(8,128)S(1)}, u32[]{:S(2)}, u32[]{:S(2)}) collective-permute-start(f32[152,512]{1,0:T(8,128)S(1)} %get-tuple-element.128), channel_id=1, source_target_pairs={{1,0},{2,1},{3,2},{0,3},{5,4},{6,5},{7,6},{4,7},{9,8},{10,9},{11,1... | collective-permute-start | bytes 933896 | tf_op jit(solution)/shard_map/ppermute | solution.py:1385
  29.4 0.0 copy-start.6
  29.4 0.0 copy-start.7
  29.5 0.0 copy-start.9
  29.5 0.0 copy-start.10
  29.5 0.0 copy-start.12
  29.5 0.0 copy-start.14
  29.5 0.0 copy-start.17
  29.5 15.0 %edges_inner.1.sums_in = f32[8000,128]{1,0:T(8,128)S(1)} custom-call(s32[16384]{0:T(1024)S(1)} %bitcast.11, s32[2048]{0:T(1024)S(1)} %bitcast.14, f32[1000,512]{1,0:T(8,128)S(1)} %get-tuple-element.110.rows_ref, f32[8,1000]{1,0:T(8,128)S(1)} %get-tuple-element.105.place_ref.p_ref, s32[16,1024]{1,0:T(8,128)S(1)} %get-tuple-element.125.table_ref, ...), custom_call_target="tpu_custom_call" | custom-call | flops 6794772480 | bytes 8192000 | tf_op jit(solution)/shard_map/edges_inner/pallas_call | solution.py:1503
  44.5 0.0 collective-permute-done.3.rest_3_
  44.6 23.2 %edges_forward.1 = (bf16[1000,128]{1,0:T(8,128)(2,1)}, bf16[1000,384]{1,0:T(8,128)(2,1)}, f32[8000,128]{1,0:T(8,128)S(1)}, f32[8,128]{1,0:T(8,128)S(1)}, f32[138...) custom-call(s32[16384]{0:T(1024)S(1)} %bitcast.12, ...), custom_call_target="tpu_custom_call" | custom-call | tf_op jit(solution)/shard_map/edges_forward/pallas_call | solution.py:1535
  67.8 2.6 %collective-permute-start.5 = (f32[224,128]{1,0:T(8,128)S(1)}, f32[224,128]{1,0:T(8,128)S(1)}, u32[]{:S(2)}, u32[]{:S(2)}) collective-permute-start(f32[224,128]{1,0:T(8,128)S(1)} %get-tuple-element.140), channel_id=1, source_target_pairs={{0,4},{4,8},{8,12},{12,0},{1,5},{5,9},{9,13},{13,1},{2,6},{6,10},{... | collective-permute-start | bytes 344072 | tf_op jit(solution)/shard_map/ppermute | solution.py:1391
  70.4 0.4 collective-permute-start.7
  70.8 58.5 %edges_backward.1 = (f32[13824,128]{1,0:T(8,128)S(1)}, f32[9,8,128]{2,1,0:T(8,128)S(1)}, f32[640,128]{1,0:T(8,128)S(1)}, f32[104,512]{1,0:T(8,128)S(1)}, f32[104...) custom-call(s32[16384]{0:T(1024)S(1)} %bitcast.13, ...), custom_call_target="tpu_custom_call" | custom-call | flops 27179089920 | bytes 8192000 | tf_op jit(solution)/shard_map/edges_backward/pallas_call | solution.py:1595
  129.4 0.1 collective-permute-start.8
  129.4 3.3 %collective-permute-start.9 = (f32[152,512]{1,0:T(8,128)S(1)}, f32[152,512]{1,0:T(8,128)S(1)}, u32[]{:S(2)}, u32[]{:S(2)}) collective-permute-start(f32[152,512]{1,0:T(8,128)S(1)} %get-tuple-element.144), channel_id=1, source_target_pairs={{1,0},{2,1},{3,2},{0,3},{5,4},{6,5},{7,6},{4,7},{9,8},{10,9},{11,1... | collective-permute-start | bytes 933896 | tf_op jit(solution)/shard_map/ppermute | solution.py:1385
  132.7 3.3 %own_backward.1 = (f32[1000,512]{1,0:T(8,128)S(1)}, f32[8,1000]{1,0:T(8,128)S(1)}, f32[224,128]{1,0:T(8,128)S(1)}, f32[160,128]{1,0:T(8,128)S(1)}, f32[160,128]{...) custom-call(s32[1]{0:T(128)} %bitcast.6.place_y.me, f32[13824,128]{1,0:T(8,128)S(1)} %get-tuple-element.145.sums, ...), custom_call_target="tpu_custom_call" | custom-call | tf_op jit(solution)/shard_map/own_backward/pallas_call | solution.py:1643
  136.0 1.3 copy-done.18
  137.3 3.5 %collective-permute-start.10 = (f32[160,128]{1,0:T(8,128)S(1)}, f32[160,128]{1,0:T(8,128)S(1)}, u32[]{:S(2)}, u32[]{:S(2)}) collective-permute-start(f32[160,128]{1,0:T(8,128)S(1)} %get-tuple-element.153), channel_id=1, source_target_pairs={{0,4},{4,8},{8,12},{12,0},{1,5},{5,9},{9,13},{13,1},{2,6},{6,10},{... | collective-permute-start | bytes 245768 | tf_op jit(solution)/shard_map/ppermute | solution.py:1391
  140.8 1.4 collective-permute-start.11
  142.3 0.3 collective-permute-done.10.refs_3_
  142.5 3.6 %collective-permute-done.11.refs_4_ = f32[160,128]{1,0:T(8,128)S(1)} collective-permute-done((f32[160,128]{1,0:T(8,128)S(1)}, f32[160,128]{1,0:T(8,128)S(1)}, u32[]{:S(2)}, u32[]{:S(2)}) %collective-permute-start.11) | collective-permute-done | bytes 81952 | tf_op jit(solution)/shard_map/ppermute | solution.py:1391
  146.2 0.6 collective-permute-done.12.refs_5_
  146.7 0.4 return_y.1
  147.1 1.6 collective-permute-start.13
  148.7 2.1 %collective-permute-start.16 = (f32[96,128]{1,0:T(8,128)S(1)}, f32[96,128]{1,0:T(8,128)S(1)}, u32[]{:S(2)}, u32[]{:S(2)}) collective-permute-start(f32[96,128]{1,0:T(8,128)S(1)} %get-tuple-element.163), channel_id=1, source_target_pairs={{0,2},{1,3},{2,0},{3,1},{4,6},{5,7},{6,4},{7,5},{8,10},{9,11},{10,... | collective-permute-start | bytes 147464 | tf_op jit(solution)/shard_map/ppermute | solution.py:1391
  150.8 2.4 %collective-permute-start.17 = (f32[96,128]{1,0:T(8,128)S(1)}, f32[96,128]{1,0:T(8,128)S(1)}, u32[]{:S(2)}, u32[]{:S(2)}) collective-permute-start(f32[96,128]{1,0:T(8,128)S(1)} %get-tuple-element.164), channel_id=1, source_target_pairs={{0,3},{1,0},{2,1},{3,2},{4,7},{5,4},{6,5},{7,6},{8,11},{9,8},{10,9... | collective-permute-start | bytes 147464 | tf_op jit(solution)/shard_map/ppermute | solution.py:1391
  153.2 1.0 collective-permute-done.15.refs_5_
  154.2 1.3 collective-permute-done.17.refs_7_
  155.5 0.5 return_x.1
  156.0 1.3 collective-permute-start.18
  157.3 1.7 collective-permute-done.18.refs_1_
  159.0 2.5 %collective-permute-start.22 = (f32[96,128]{1,0:T(8,128)S(1)}, f32[96,128]{1,0:T(8,128)S(1)}, u32[]{:S(2)}, u32[]{:S(2)}) collective-permute-start(f32[96,128]{1,0:T(8,128)S(1)} %sum_last.1.refs_0_), channel_id=1, source_target_pairs={{0,3},{1,0},{2,1},{3,2},{4,7},{5,4},{6,5},{7,6},{8,11},{9,8},{10,9... | collective-permute-start | bytes 147464 | tf_op jit(solution)/shard_map/ppermute | solution.py:1391
  161.5 0.1 collective-permute-start.21
  161.5 0.5 collective-permute-start.20
  162.0 1.9 %collective-permute-start.19 = (f32[208,512]{1,0:T(8,128)S(1)}, f32[208,512]{1,0:T(8,128)S(1)}, u32[]{:S(2)}, u32[]{:S(2)}) collective-permute-start(f32[208,512]{1,0:T(8,128)S(1)} %get-tuple-element.169), channel_id=1, source_target_pairs={{0,16},{16,0},{1,17},{17,1},{2,18},{18,2},{3,19},{19,3},{4,20},{20... | collective-permute-start | bytes 1277960 | tf_op jit(solution)/shard_map/ppermute | solution.py:1383
  163.9 1.4 own_partial.1
  165.3 0.4 collective-permute-done.21.refs_2_
  165.7 0.7 collective-permute-done.20.refs_1_
  166.4 0.9 collective-permute-start.24
  167.3 5.4 %collective-permute-start.23 = (f32[384,128]{1,0:T(8,128)S(1)}, f32[384,128]{1,0:T(8,128)S(1)}, u32[]{:S(2)}, u32[]{:S(2)}) collective-permute-start(f32[384,128]{1,0:T(8,128)S(1)} %join_shares.1.refs_0_), channel_id=1, source_target_pairs={{0,4},{4,0},{8,12},{12,8},{1,5},{5,1},{9,13},{13,9},{2,6},{6,2},{1... | collective-permute-start | bytes 589832 | tf_op jit(solution)/shard_map/ppermute | solution.py:1401
  172.7 3.6 %collective-permute-start.25 = (f32[384,128]{1,0:T(8,128)S(1)}, f32[384,128]{1,0:T(8,128)S(1)}, u32[]{:S(2)}, u32[]{:S(2)}) collective-permute-start(f32[384,128]{1,0:T(8,128)S(1)} %collective-permute-done.24.refs_2_), channel_id=1, source_target_pairs={{0,4},{4,0},{8,12},{12,8},{1,5},{5,1},{9,13},{13,9},{2,6},{6,2},{1... | collective-permute-start | bytes 589832 | tf_op jit(solution)/shard_map/ppermute | solution.py:1402
  176.4 1.9 %own_last.1 = (f32[1000,128]{1,0:T(8,128)}, f32[1000,384]{1,0:T(8,128)}, f32[3,1000]{1,0:T(4,128)}) custom-call(s32[2,100]{1,0:T(2,128)S(1)} %bitcast.22, f32[208,512]{1,0:T(8,128)S(1)} %collective-permute-done.19.refs_1_, f32[1000,512]{1,0:T(8,128)S(1)} %get-tuple-element.175.refs_2_, f32[8,1000]{1,0:T(8,128)S(1)} %get-tuple-element.176.refs_3_), custom_call_target="tpu_custom_call" | custom-call | flops 409600000 | bytes 8192000 | tf_op jit(solution)/shard_map/own_last/pallas_call | solution.py:1705
  178.3 0.9 unpack_weights.1
  (54 shorter events, 0.1 us)
Async XLA Ops:
  0.7 18.3 %copy-start.20 = (f32[384]{0:T(512)S(1)}, f32[384]{0:T(512)}, u32[]{:S(2)}) copy-start(f32[384]{0:T(512)} %param.30) | copy-start | bytes 4612
  0.7 18.3 %copy-start.21 = (f32[384]{0:T(512)S(1)}, f32[384]{0:T(512)}, u32[]{:S(2)}) copy-start(f32[384]{0:T(512)} %param.32) | copy-start | bytes 4612
  0.7 18.3 %copy-start.22 = (f32[384]{0:T(512)S(1)}, f32[384]{0:T(512)}, u32[]{:S(2)}) copy-start(f32[384]{0:T(512)} %param.38) | copy-start | bytes 4612
  2.8 11.6 %collective-permute-start = (f32[208,512]{1,0:T(8,128)S(1)}, f32[208,512]{1,0:T(8,128)S(1)}, u32[]{:S(2)}, u32[]{:S(2)}) collective-permute-start(f32[208,512]{1,0:T(8,128)S(1)} %get-tuple-element.113), channel_id=1, source_target_pairs={{0,16},{16,0},{1,17},{17,1},{2,18},{18,2},{3,19},{19,3},{4,20},{20... | collective-permute-start | bytes 1277960 | tf_op jit(solution)/shard_map/ppermute | solution.py:1383
  4.9 0.8 copy-start.8
  5.7 0.7 copy-start.11
  9.4 6.2 %copy-start.3 = (f32[152,512]{1,0:T(8,128)}, f32[152,512]{1,0:T(8,128)S(1)}, u32[]{:S(2)}) copy-start(f32[152,512]{1,0:T(8,128)S(1)} %get-tuple-element.112.own_upper) | copy-start | bytes 933892
  15.6 8.6 %collective-permute-start.1 = (f32[128,512]{1,0:T(8,128)}, f32[128,512]{1,0:T(8,128)S(1)}, u32[]{:S(2)}, u32[]{:S(2)}) collective-permute-start(f32[128,512]{1,0:T(8,128)} %get-tuple-element.119), channel_id=1, source_target_pairs={{0,4},{4,8},{8,12},{12,0},{1,5},{5,9},{9,13},{13,1},{2,6},{6,10},{... | collective-permute-start | bytes 786440 | tf_op jit(solution)/shard_map/ppermute | solution.py:1385
  18.2 6.7 %collective-permute-start.2 = (f32[128,512]{1,0:T(8,128)}, f32[128,512]{1,0:T(8,128)S(1)}, u32[]{:S(2)}, u32[]{:S(2)}) collective-permute-start(f32[128,512]{1,0:T(8,128)} %get-tuple-element.120), channel_id=1, source_target_pairs={{4,0},{8,4},{12,8},{0,12},{5,1},{9,5},{13,9},{1,13},{6,2},{10,6},{... | collective-permute-start | bytes 786440 | tf_op jit(solution)/shard_map/ppermute | solution.py:1385
  18.2 6.7 %copy-start.4 = (f32[152,512]{1,0:T(8,128)S(1)}, f32[152,512]{1,0:T(8,128)}, u32[]{:S(2)}) copy-start(f32[152,512]{1,0:T(8,128)} %copy-done.3) | copy-start | bytes 933892
  19.0 10.4 %copy-start.2 = (bf16[128,384]{1,0:T(8,128)(2,1)S(1)}, bf16[128,384]{1,0:T(8,128)(2,1)}, u32[]{:S(2)}) copy-start(bf16[128,384]{1,0:T(8,128)(2,1)} %w2_ref.7) | copy-start | bytes 294916
  19.0 10.4 %copy-start.5 = (bf16[128,128]{1,0:T(8,128)(2,1)S(1)}, bf16[128,128]{1,0:T(8,128)(2,1)}, u32[]{:S(2)}) copy-start(bf16[128,128]{1,0:T(8,128)(2,1)} %w1_ref.7) | copy-start | bytes 98308
  19.0 10.4 %copy-start.13 = (bf16[20,384]{1,0:T(8,128)(2,1)S(1)}, bf16[20,384]{1,0:T(8,128)(2,1)}, u32[]{:S(2)}) copy-start(bf16[20,384]{1,0:T(8,128)(2,1)} %wr_ref.5) | copy-start | bytes 46084
  19.0 10.4 %copy-start.16 = (f32[128]{0:T(128)S(1)}, f32[128]{0:T(128)}, u32[]{:S(2)}) copy-start(f32[128]{0:T(128)} %param.28) | copy-start | bytes 1540
  25.7 18.8 %collective-permute-start.3 = (f32[152,512]{1,0:T(8,128)S(1)}, f32[152,512]{1,0:T(8,128)S(1)}, u32[]{:S(2)}, u32[]{:S(2)}) collective-permute-start(f32[152,512]{1,0:T(8,128)S(1)} %get-tuple-element.127), channel_id=1, source_target_pairs={{0,1},{1,2},{2,3},{3,0},{4,5},{5,6},{6,7},{7,4},{8,9},{9,10},{10,1... | collective-permute-start | bytes 933896 | tf_op jit(solution)/shard_map/ppermute | solution.py:1385
  27.3 17.2 %collective-permute-start.4 = (f32[152,512]{1,0:T(8,128)S(1)}, f32[152,512]{1,0:T(8,128)S(1)}, u32[]{:S(2)}, u32[]{:S(2)}) collective-permute-start(f32[152,512]{1,0:T(8,128)S(1)} %get-tuple-element.128), channel_id=1, source_target_pairs={{1,0},{2,1},{3,2},{0,3},{5,4},{6,5},{7,6},{4,7},{9,8},{10,9},{11,1... | collective-permute-start | bytes 933896 | tf_op jit(solution)/shard_map/ppermute | solution.py:1385
  29.4 15.1 %copy-start.6 = (bf16[128,384]{1,0:T(8,128)(2,1)S(1)}, bf16[128,384]{1,0:T(8,128)(2,1)}, u32[]{:S(2)}) copy-start(bf16[128,384]{1,0:T(8,128)(2,1)} %w4_ref.1) | copy-start | bytes 294916
  29.4 15.1 %copy-start.7 = (bf16[256,128]{1,0:T(8,128)(2,1)S(1)}, bf16[256,128]{1,0:T(8,128)(2,1)}, u32[]{:S(2)}) copy-start(bf16[256,128]{1,0:T(8,128)(2,1)} %w3_ref.1) | copy-start | bytes 196612
  29.5 15.1 %copy-start.9 = (bf16[128,128]{1,0:T(8,128)(2,1)S(1)}, bf16[128,128]{1,0:T(8,128)(2,1)}, u32[]{:S(2)}) copy-start(bf16[128,128]{1,0:T(8,128)(2,1)} %u_ref.1) | copy-start | bytes 98308
  29.5 15.1 %copy-start.10 = (bf16[128,128]{1,0:T(8,128)(2,1)S(1)}, bf16[128,128]{1,0:T(8,128)(2,1)}, u32[]{:S(2)}) copy-start(bf16[128,128]{1,0:T(8,128)(2,1)} %v_ref.2) | copy-start | bytes 98308
  29.5 15.1 %copy-start.12 = (s32[11,128]{1,0:T(8,128)S(1)}, s32[11,128]{1,0:T(8,128)}, u32[]{:S(2)}) copy-start(s32[11,128]{1,0:T(8,128)} %hub_table_ref.3) | copy-start | bytes 16900
  29.5 15.1 %copy-start.14 = (s32[128]{0:T(128)S(1)}, s32[128]{0:T(128)}, u32[]{:S(2)}) copy-start(s32[128]{0:T(128)} %hub_list.3) | copy-start | bytes 1540
  29.5 15.1 %copy-start.17 = (f32[128]{0:T(128)S(1)}, f32[128]{0:T(128)}, u32[]{:S(2)}) copy-start(f32[128]{0:T(128)} %param.36) | copy-start | bytes 1540
  67.8 61.6 %collective-permute-start.5 = (f32[224,128]{1,0:T(8,128)S(1)}, f32[224,128]{1,0:T(8,128)S(1)}, u32[]{:S(2)}, u32[]{:S(2)}) collective-permute-start(f32[224,128]{1,0:T(8,128)S(1)} %get-tuple-element.140), channel_id=1, source_target_pairs={{0,4},{4,8},{8,12},{12,0},{1,5},{5,9},{9,13},{13,1},{2,6},{6,10},{... | collective-permute-start | bytes 344072 | tf_op jit(solution)/shard_map/ppermute | solution.py:1391
  70.4 58.9 %collective-permute-start.6 = (f32[224,128]{1,0:T(8,128)S(1)}, f32[224,128]{1,0:T(8,128)S(1)}, u32[]{:S(2)}, u32[]{:S(2)}) collective-permute-start(f32[224,128]{1,0:T(8,128)S(1)} %get-tuple-element.141), channel_id=1, source_target_pairs={{0,8},{4,12},{8,0},{12,4},{1,9},{5,13},{9,1},{13,5},{2,10},{6,14},... | collective-permute-start | bytes 344072 | tf_op jit(solution)/shard_map/ppermute | solution.py:1391
  70.4 58.9 %collective-permute-start.7 = (f32[224,128]{1,0:T(8,128)S(1)}, f32[224,128]{1,0:T(8,128)S(1)}, u32[]{:S(2)}, u32[]{:S(2)}) collective-permute-start(f32[224,128]{1,0:T(8,128)S(1)} %get-tuple-element.142), channel_id=1, source_target_pairs={{0,12},{4,0},{8,4},{12,8},{1,13},{5,1},{9,5},{13,9},{2,14},{6,2},{... | collective-permute-start | bytes 344072 | tf_op jit(solution)/shard_map/ppermute | solution.py:1391
  70.8 61.8 %copy-start = (bf16[1000,384]{1,0:T(8,128)(2,1)S(1)}, bf16[1000,384]{1,0:T(8,128)(2,1)}, u32[]{:S(2)}) copy-start(bf16[1000,384]{1,0:T(8,128)(2,1)} %v_ref.3) | copy-start | bytes 2304004
  70.8 61.8 %copy-start.1 = (bf16[1000,128]{1,0:T(8,128)(2,1)S(1)}, bf16[1000,128]{1,0:T(8,128)(2,1)}, u32[]{:S(2)}) copy-start(bf16[1000,128]{1,0:T(8,128)(2,1)} %s_ref.1) | copy-start | bytes 768004
  129.4 17.4 %collective-permute-start.8 = (f32[152,512]{1,0:T(8,128)}, f32[152,512]{1,0:T(8,128)S(1)}, u32[]{:S(2)}, u32[]{:S(2)}) collective-permute-start(f32[152,512]{1,0:T(8,128)} %get-tuple-element.143), channel_id=1, source_target_pairs={{0,1},{1,2},{2,3},{3,0},{4,5},{5,6},{6,7},{7,4},{8,9},{9,10},{10,1... | collective-permute-start | bytes 933896 | tf_op jit(solution)/shard_map/ppermute | solution.py:1385
  129.4 17.3 %collective-permute-start.9 = (f32[152,512]{1,0:T(8,128)S(1)}, f32[152,512]{1,0:T(8,128)S(1)}, u32[]{:S(2)}, u32[]{:S(2)}) collective-permute-start(f32[152,512]{1,0:T(8,128)S(1)} %get-tuple-element.144), channel_id=1, source_target_pairs={{1,0},{2,1},{3,2},{0,3},{5,4},{6,5},{7,6},{4,7},{9,8},{10,9},{11,1... | collective-permute-start | bytes 933896 | tf_op jit(solution)/shard_map/ppermute | solution.py:1385
  135.9 1.4 copy-start.18
  137.3 5.2 %collective-permute-start.10 = (f32[160,128]{1,0:T(8,128)S(1)}, f32[160,128]{1,0:T(8,128)S(1)}, u32[]{:S(2)}, u32[]{:S(2)}) collective-permute-start(f32[160,128]{1,0:T(8,128)S(1)} %get-tuple-element.153), channel_id=1, source_target_pairs={{0,4},{4,8},{8,12},{12,0},{1,5},{5,9},{9,13},{13,1},{2,6},{6,10},{... | collective-permute-start | bytes 245768 | tf_op jit(solution)/shard_map/ppermute | solution.py:1391
  140.8 5.3 %collective-permute-start.11 = (f32[160,128]{1,0:T(8,128)S(1)}, f32[160,128]{1,0:T(8,128)S(1)}, u32[]{:S(2)}, u32[]{:S(2)}) collective-permute-start(f32[160,128]{1,0:T(8,128)S(1)} %get-tuple-element.154), channel_id=1, source_target_pairs={{0,8},{4,12},{8,0},{12,4},{1,9},{5,13},{9,1},{13,5},{2,10},{6,14},... | collective-permute-start | bytes 245768 | tf_op jit(solution)/shard_map/ppermute | solution.py:1391
  142.3 4.5 %collective-permute-start.12 = (f32[160,128]{1,0:T(8,128)S(1)}, f32[160,128]{1,0:T(8,128)S(1)}, u32[]{:S(2)}, u32[]{:S(2)}) collective-permute-start(f32[160,128]{1,0:T(8,128)S(1)} %get-tuple-element.155), channel_id=1, source_target_pairs={{0,12},{4,0},{8,4},{12,8},{1,13},{5,1},{9,5},{13,9},{2,14},{6,2},{... | collective-permute-start | bytes 245768 | tf_op jit(solution)/shard_map/ppermute | solution.py:1391
  142.3 21.6 %copy-start.19 = (f32[1000,512]{1,0:T(8,128)S(1)}, f32[1000,512]{1,0:T(8,128)}, u32[]{:S(2)}) copy-start(f32[1000,512]{1,0:T(8,128)} %copy-done.18) | copy-start | bytes 6144004
  147.1 8.3 %collective-permute-start.13 = (f32[128,512]{1,0:T(8,128)S(1)}, f32[128,512]{1,0:T(8,128)S(1)}, u32[]{:S(2)}, u32[]{:S(2)}) collective-permute-start(f32[128,512]{1,0:T(8,128)S(1)} %get-tuple-element.159), channel_id=1, source_target_pairs={{0,4},{4,8},{8,12},{12,0},{1,5},{5,9},{9,13},{13,1},{2,6},{6,10},{... | collective-permute-start | bytes 786440 | tf_op jit(solution)/shard_map/ppermute | solution.py:1385
  148.7 6.7 %collective-permute-start.14 = (f32[128,512]{1,0:T(8,128)S(1)}, f32[128,512]{1,0:T(8,128)S(1)}, u32[]{:S(2)}, u32[]{:S(2)}) collective-permute-start(f32[128,512]{1,0:T(8,128)S(1)} %get-tuple-element.160), channel_id=1, source_target_pairs={{4,0},{8,4},{12,8},{0,12},{5,1},{9,5},{13,9},{1,13},{6,2},{10,6},{... | collective-permute-start | bytes 786440 | tf_op jit(solution)/shard_map/ppermute | solution.py:1385
  148.7 5.4 %collective-permute-start.15 = (f32[96,128]{1,0:T(8,128)S(1)}, f32[96,128]{1,0:T(8,128)S(1)}, u32[]{:S(2)}, u32[]{:S(2)}) collective-permute-start(f32[96,128]{1,0:T(8,128)S(1)} %get-tuple-element.162), channel_id=1, source_target_pairs={{0,1},{1,2},{2,3},{3,0},{4,5},{5,6},{6,7},{7,4},{8,9},{9,10},{10,1... | collective-permute-start | bytes 147464 | tf_op jit(solution)/shard_map/ppermute | solution.py:1391
  148.7 5.4 %collective-permute-start.16 = (f32[96,128]{1,0:T(8,128)S(1)}, f32[96,128]{1,0:T(8,128)S(1)}, u32[]{:S(2)}, u32[]{:S(2)}) collective-permute-start(f32[96,128]{1,0:T(8,128)S(1)} %get-tuple-element.163), channel_id=1, source_target_pairs={{0,2},{1,3},{2,0},{3,1},{4,6},{5,7},{6,4},{7,5},{8,10},{9,11},{10,... | collective-permute-start | bytes 147464 | tf_op jit(solution)/shard_map/ppermute | solution.py:1391
  150.8 4.7 %collective-permute-start.17 = (f32[96,128]{1,0:T(8,128)S(1)}, f32[96,128]{1,0:T(8,128)S(1)}, u32[]{:S(2)}, u32[]{:S(2)}) collective-permute-start(f32[96,128]{1,0:T(8,128)S(1)} %get-tuple-element.164), channel_id=1, source_target_pairs={{0,3},{1,0},{2,1},{3,2},{4,7},{5,4},{6,5},{7,6},{8,11},{9,8},{10,9... | collective-permute-start | bytes 147464 | tf_op jit(solution)/shard_map/ppermute | solution.py:1391
  156.0 3.0 %collective-permute-start.18 = (f32[96,128]{1,0:T(8,128)S(1)}, f32[96,128]{1,0:T(8,128)S(1)}, u32[]{:S(2)}, u32[]{:S(2)}) collective-permute-start(f32[96,128]{1,0:T(8,128)S(1)} %get-tuple-element.168.refs_0_), channel_id=1, source_target_pairs={{0,16},{16,0},{1,17},{17,1},{2,18},{18,2},{3,19},{19,3},{4,20},{20... | collective-permute-start | bytes 147464 | tf_op jit(solution)/shard_map/ppermute | solution.py:1391
  159.0 6.3 %collective-permute-start.22 = (f32[96,128]{1,0:T(8,128)S(1)}, f32[96,128]{1,0:T(8,128)S(1)}, u32[]{:S(2)}, u32[]{:S(2)}) collective-permute-start(f32[96,128]{1,0:T(8,128)S(1)} %sum_last.1.refs_0_), channel_id=1, source_target_pairs={{0,3},{1,0},{2,1},{3,2},{4,7},{5,4},{6,5},{7,6},{8,11},{9,8},{10,9... | collective-permute-start | bytes 147464 | tf_op jit(solution)/shard_map/ppermute | solution.py:1391
  161.5 4.2 %collective-permute-start.21 = (f32[96,128]{1,0:T(8,128)S(1)}, f32[96,128]{1,0:T(8,128)S(1)}, u32[]{:S(2)}, u32[]{:S(2)}) collective-permute-start(f32[96,128]{1,0:T(8,128)S(1)} %sum_last.1.refs_0_), channel_id=1, source_target_pairs={{0,2},{1,3},{2,0},{3,1},{4,6},{5,7},{6,4},{7,5},{8,10},{9,11},{10,... | collective-permute-start | bytes 147464 | tf_op jit(solution)/shard_map/ppermute | solution.py:1391
  161.5 4.8 %collective-permute-start.20 = (f32[96,128]{1,0:T(8,128)S(1)}, f32[96,128]{1,0:T(8,128)S(1)}, u32[]{:S(2)}, u32[]{:S(2)}) collective-permute-start(f32[96,128]{1,0:T(8,128)S(1)} %sum_last.1.refs_0_), channel_id=1, source_target_pairs={{0,1},{1,2},{2,3},{3,0},{4,5},{5,6},{6,7},{7,4},{8,9},{9,10},{10,1... | collective-permute-start | bytes 147464 | tf_op jit(solution)/shard_map/ppermute | solution.py:1391
  162.0 14.4 %collective-permute-start.19 = (f32[208,512]{1,0:T(8,128)S(1)}, f32[208,512]{1,0:T(8,128)S(1)}, u32[]{:S(2)}, u32[]{:S(2)}) collective-permute-start(f32[208,512]{1,0:T(8,128)S(1)} %get-tuple-element.169), channel_id=1, source_target_pairs={{0,16},{16,0},{1,17},{17,1},{2,18},{18,2},{3,19},{19,3},{4,20},{20... | collective-permute-start | bytes 1277960 | tf_op jit(solution)/shard_map/ppermute | solution.py:1383
  163.9 12.5 %copy-start.15 = (s32[1,2,100]{2,1,0:T(2,128)S(1)}, s32[1,2,100]{2,1,0:T(2,128)}, u32[]{:S(2)}) copy-start(s32[1,2,100]{2,1,0:T(2,128)} %param.41) | copy-start | bytes 2404
  166.4 6.3 %collective-permute-start.24 = (f32[384,128]{1,0:T(8,128)S(1)}, f32[384,128]{1,0:T(8,128)S(1)}, u32[]{:S(2)}, u32[]{:S(2)}) collective-permute-start(f32[384,128]{1,0:T(8,128)S(1)} %join_shares.1.refs_0_), channel_id=1, source_target_pairs={{0,8},{4,12},{8,0},{12,4},{1,9},{5,13},{9,1},{13,5},{2,10},{6,14},... | collective-permute-start | bytes 589832 | tf_op jit(solution)/shard_map/ppermute | solution.py:1400
  167.3 11.0 %collective-permute-start.23 = (f32[384,128]{1,0:T(8,128)S(1)}, f32[384,128]{1,0:T(8,128)S(1)}, u32[]{:S(2)}, u32[]{:S(2)}) collective-permute-start(f32[384,128]{1,0:T(8,128)S(1)} %join_shares.1.refs_0_), channel_id=1, source_target_pairs={{0,4},{4,0},{8,12},{12,8},{1,5},{5,1},{9,13},{13,9},{2,6},{6,2},{1... | collective-permute-start | bytes 589832 | tf_op jit(solution)/shard_map/ppermute | solution.py:1401
  172.7 5.6 %collective-permute-start.25 = (f32[384,128]{1,0:T(8,128)S(1)}, f32[384,128]{1,0:T(8,128)S(1)}, u32[]{:S(2)}, u32[]{:S(2)}) collective-permute-start(f32[384,128]{1,0:T(8,128)S(1)} %collective-permute-done.24.refs_2_), channel_id=1, source_target_pairs={{0,4},{4,0},{8,12},{12,8},{1,5},{5,1},{9,13},{13,9},{2,6},{6,2},{1... | collective-permute-start | bytes 589832 | tf_op jit(solution)/shard_map/ppermute | solution.py:1402
